TPU v7x, 32 devices: a whole 2x2x4 slice. The times are simulated.
32 devices in a mesh: side: 2 (over x), grp: 4 (over z), blk: 4 (over y, core).
Axes of the slice: x: 2, y: 2, z: 4, core: 2. Of those that a mesh axis runs over, the one named last changes fastest.
Arguments:
- embed_codes: bfloat16 [2, 8192, 128], P('side', ('grp', 'blk')), may hold values from -4 to 4
- embed_exps: int32 [2, 64], P('side', ('grp', 'blk')), may hold values from -1 to 1
- degrees: int32 [2, 8192], P('side', ('grp', 'blk')), may hold values from 16 to 128
- adjacency: bfloat16 [2, 1536, 128, 128], P('side', ('grp', 'blk')), may hold values from 0 to 1
- block_index: int32 [2, 2, 1536], P('side', None, ('grp', 'blk')), may hold values from 0 to 16, as said below
Outputs:
- layer_rows: bfloat16 [2, 8192, 128], P('side', ('grp', 'blk'))
Inputs may be any that keep to these rules, and one draw needn't show every extreme that they name: `block_index`: each device's list of 96 slots: its used slots come first, in non-decreasing source tile (row 1 below 16), with distinct (destination, source) pairs and destination tiles below 16; the remaining slots have source 16 and destination 0. Every list uses 96 // 4 slots or more, and in each section one list uses all 96.
All inputs are finite; a program needn't handle non-finite values.
Results may differ from a plain program's by a relative error of at most 0.0048.
Values may be sent and summed in bfloat16 or wider, within the bound.
No kernel may reach another device: no remote copies, remote signals or barrier semaphores. Data moves between devices by JAX's collectives and lax.ppermute only.
A program may use at most 128 MiB of HBM per device.

v0:
```python
import functools

import jax
import jax.numpy as jnp
from jax import lax
from jax.experimental import pallas as pl
from jax.experimental.pallas import tpu as pltpu
from jax.sharding import PartitionSpec as P

UNROLL = 8
STAGES = 4
VMEM = pl.BlockSpec(memory_space=pltpu.VMEM)
SMEM = pl.BlockSpec(memory_space=pltpu.SMEM)
HBM = pl.BlockSpec(memory_space=pltpu.HBM)
LIMIT = pltpu.CompilerParams(vmem_limit_bytes=48 * 1024 * 1024)


def in_hbm(*arrays):
    return [pltpu.with_memory_space_constraint(array, pltpu.HBM) for array in arrays]


def split(value, size):
    if size & (size - 1) == 0:
        return value >> (size.bit_length() - 1), value & (size - 1)
    return value // size, value % size


def scale_kernel(exps_hbm, degrees_hbm, codes_hbm, rows, exps_ref, degrees, codes, sems):
    pairs = [(exps_hbm, exps_ref), (degrees_hbm, degrees), (codes_hbm, codes)]
    fetches = [
        pltpu.make_async_copy(held, wanted, sems.at[at])
        for at, (held, wanted) in enumerate(pairs)
    ]
    for fetch in fetches:
        fetch.start()
    fetches[0].wait()
    fetches[1].wait()
    tiles_dev, tile_rows, row_width = rows.shape
    inverse = lax.rsqrt(degrees[...].astype(jnp.float32))
    factors = []
    for tile in range(tiles_dev):
        lanes = inverse[:, tile * tile_rows : (tile + 1) * tile_rows]
        scale = jnp.exp2(jnp.full(lanes.shape, exps_ref[0, tile], jnp.int32).astype(jnp.float32))
        factors.append(jnp.broadcast_to(lanes * scale, (row_width, tile_rows)).T)
    fetches[2].wait()
    for tile, factor in enumerate(factors):
        rows[tile] = (codes[tile].astype(jnp.float32) * factor).astype(rows.dtype)


def scale_rows(codes, exps, degrees):
    return pl.pallas_call(
        scale_kernel,
        out_shape=jax.ShapeDtypeStruct(codes.shape, jnp.bfloat16),
        in_specs=[HBM] * 3,
        out_specs=VMEM,
        scratch_shapes=[
            pltpu.SMEM(exps.shape, exps.dtype),
            pltpu.VMEM(degrees.shape, degrees.dtype),
            pltpu.VMEM(codes.shape, codes.dtype),
            pltpu.SemaphoreType.DMA((3,)),
        ],
        compiler_params=LIMIT,
        cost_estimate=pl.CostEstimate(
            flops=codes.size, bytes_accessed=4 * codes.size, transcendentals=0
        ),
    )(*in_hbm(exps, degrees, codes))


def stage_kernel(
    blks, groups, tiles_dev, place_ref, index_hbm, blocks_hbm, order_ref, blocks, index_ref, sems
):
    fetch = pltpu.make_async_copy(index_hbm, index_ref, sems.at[0])
    fetch.start()
    copy = pltpu.make_async_copy(blocks_hbm, blocks, sems.at[1])
    copy.start()
    fetch.wait()
    my_blk = place_ref[0]
    my_grp = place_ref[1]
    capacity = index_ref.shape[1]
    source_tiles = blks * tiles_dev
    half = blks // 2

    def enlist(slot, nexts):
        target = index_ref[0, slot]
        origin = index_ref[1, slot]
        hop, row = split(origin, tiles_dev)
        chunk, tile = split(target, tiles_dev)
        hop = hop ^ my_blk
        chunk = chunk ^ my_grp
        rank = half - 1 - (hop >> 1)
        odd = hop & 1
        far = (chunk >= 2) & ((chunk & 1) == 1)
        first = (odd == 0) & (rank == 0)
        last = (odd == 1) & (rank > 0)
        stage = jnp.where(first, 0, jnp.where(far, jnp.where(last, 2, 1), 3))
        stage = jnp.where(origin < source_tiles, stage, STAGES)
        panel = jnp.where(odd == 1, jnp.where(rank == 0, half - 1, rank - 1), rank - 1)
        panel = jnp.where(last & (stage == 3), panel + half, jnp.maximum(panel, 0))
        word = pack(slot, panel * tiles_dev + row, chunk * tiles_dev + tile)
        where = jnp.int32(0)
        for at, position in enumerate(nexts):
            where = jnp.where(stage == at, position, where)
        order_ref[stage, where] = word
        return tuple(
            position + (stage == at).astype(jnp.int32) for at, position in enumerate(nexts)
        )

    ends = lax.fori_loop(0, capacity, enlist, (jnp.int32(0),) * STAGES, unroll=8)
    spare = pack(0, 0, groups * tiles_dev)
    for at, end in enumerate(ends):
        for extra in range(UNROLL):
            order_ref[at, end + extra] = spare
        order_ref[at, capacity + UNROLL] = split(end + (UNROLL - 1), UNROLL)[0]
    copy.wait()


def pack(slot, row, target):
    return (slot << 16) | (row << 8) | target


def unpack(word):
    return word >> 16, (word >> 8) & 255, word & 255


def stage_blocks(index, place, blocks, blks, groups, tiles_dev):
    capacity = blocks.shape[0]
    assert blks * tiles_dev < 256 and groups * tiles_dev < 256 and capacity < 2**15
    return pl.pallas_call(
        functools.partial(stage_kernel, blks, groups, tiles_dev),
        out_shape=[
            jax.ShapeDtypeStruct((STAGES + 1, capacity + 2 * UNROLL), jnp.int32),
            jax.ShapeDtypeStruct(blocks.shape, blocks.dtype),
        ],
        in_specs=[SMEM, HBM, HBM],
        out_specs=[SMEM, VMEM],
        scratch_shapes=[
            pltpu.SMEM(index.shape, index.dtype),
            pltpu.SemaphoreType.DMA((2,)),
        ],
        compiler_params=LIMIT,
        cost_estimate=pl.CostEstimate(flops=0, bytes_accessed=0, transcendentals=0),
    )(place, *in_hbm(index, blocks))


def add_products(stage, order_ref, blocks, source, total):
    @pl.loop(0, order_ref[stage, order_ref.shape[1] - UNROLL])
    def _(batch):
        made = []
        for part in range(UNROLL):
            slot, row, target = unpack(order_ref[stage, batch * UNROLL + part])
            product = jnp.dot(blocks[slot], source[row], preferred_element_type=jnp.float32)
            made.append((target, product))
        for target, product in made:
            total[target] += product


def gather_panels(panels, source):
    for at, panel in enumerate(panels):
        rows = panel.shape[0]
        source[at * rows : (at + 1) * rows] = panel[...]


def first_kernel(order_ref, panel, blocks, total):
    total[...] = jnp.zeros_like(total)
    add_products(0, order_ref, blocks, panel, total)


def second_kernel(order_ref, *refs):
    *panels, blocks, _, total, source = refs
    gather_panels(panels, source)
    add_products(1, order_ref, blocks, source, total)


def far_kernel(tiles_dev, chunks, order_ref, *refs):
    *panels, blocks, _, far, total, source = refs
    gather_panels(panels, source)
    add_products(2, order_ref, blocks, source, total)
    for at, chunk in enumerate(chunks):
        far[at] = total[chunk * tiles_dev : (chunk + 1) * tiles_dev].astype(far.dtype)


def near_kernel(tiles_dev, chunks, order_ref, *refs):
    *panels, blocks, total, own, near, mine, source = refs
    gather_panels(panels, source)
    add_products(3, order_ref, blocks, source, total)
    own[...] = total[:tiles_dev]
    near[...] = total[tiles_dev : 2 * tiles_dev].astype(near.dtype)
    for at, chunk in enumerate(chunks):
        mine[at] = total[chunk * tiles_dev : (chunk + 1) * tiles_dev]


def cost_of(slots, tile_rows, row_width):
    return pl.CostEstimate(
        flops=2 * slots * tile_rows * tile_rows * row_width,
        bytes_accessed=2 * slots * tile_rows * tile_rows,
        transcendentals=0,
    )


def shards(embed_codes, embed_exps, degrees, adjacency, block_index):
    tile_rows = adjacency.shape[2]
    row_width = embed_codes.shape[2]
    row_count = embed_codes.shape[1]
    capacity = adjacency.shape[1]
    tiles_dev = row_count // tile_rows
    groups = lax.axis_size("grp")
    blks = lax.axis_size("blk")
    part = (tiles_dev, tile_rows, row_width)
    dest_tiles = groups * tiles_dev
    source = scale_rows(embed_codes.reshape(part), embed_exps, degrees)

    def across(value, hop):
        pairs = [
            (side * blks + at, (1 - side) * blks + (at ^ hop))
            for side in range(2)
            for at in range(blks)
        ]
        return lax.ppermute(value, ("side", "blk"), pairs)

    def paired(value, axis, hop):
        return lax.ppermute(value, axis, [(at, at ^ hop) for at in range(lax.axis_size(axis))])

    place = jnp.stack([lax.axis_index("blk"), lax.axis_index("grp")]).astype(jnp.int32)
    early, *middle = [across(source, hop) for hop in reversed(range(0, blks, 2))]
    order, blocks = stage_blocks(block_index[0], place, adjacency[0], blks, groups, tiles_dev)
    early, order = lax.optimization_barrier((early, order))
    total_shape = jax.ShapeDtypeStruct((dest_tiles + 1, tile_rows, row_width), jnp.float32)
    total = pl.pallas_call(
        first_kernel,
        out_shape=total_shape,
        in_specs=[SMEM] + [VMEM] * 2,
        out_specs=VMEM,
        compiler_params=LIMIT,
        cost_estimate=cost_of(capacity // 4, tile_rows, row_width),
    )(order, early, blocks)
    other = paired(early, "blk", 1)
    *middle, total = lax.optimization_barrier((*middle, total))
    last = [paired(panel, "blk", 1) for panel in middle]
    middle += [other]
    total = pl.pallas_call(
        second_kernel,
        out_shape=total_shape,
        in_specs=[SMEM] + [VMEM] * (len(middle) + 2),
        out_specs=VMEM,
        input_output_aliases={len(middle) + 2: 0},
        scratch_shapes=[
            pltpu.VMEM((len(middle) * tiles_dev, tile_rows, row_width), jnp.bfloat16)
        ],
        compiler_params=LIMIT,
        cost_estimate=cost_of(capacity // 4, tile_rows, row_width),
    )(order, *middle, blocks, total)
    *last, total = lax.optimization_barrier((*last, total))
    far_chunks = range(3, groups, 2)
    far, total = pl.pallas_call(
        functools.partial(far_kernel, tiles_dev, far_chunks),
        out_shape=[
            jax.ShapeDtypeStruct((len(far_chunks),) + part, jnp.bfloat16),
            total_shape,
        ],
        in_specs=[SMEM] + [VMEM] * (len(last) + 2),
        out_specs=[VMEM, VMEM],
        input_output_aliases={len(last) + 2: 1},
        scratch_shapes=[
            pltpu.VMEM((len(last) * tiles_dev, tile_rows, row_width), jnp.bfloat16)
        ],
        compiler_params=LIMIT,
        cost_estimate=cost_of(capacity // 8, tile_rows, row_width),
    )(order, *last, blocks, total)
    far_arrived = paired(far, "grp", 1)
    mine_chunks = range(2, groups, 2)
    own, near, mine = pl.pallas_call(
        functools.partial(near_kernel, tiles_dev, mine_chunks),
        out_shape=[
            jax.ShapeDtypeStruct(part, jnp.float32),
            jax.ShapeDtypeStruct(part, jnp.bfloat16),
            jax.ShapeDtypeStruct((len(mine_chunks),) + part, jnp.float32),
        ],
        in_specs=[SMEM] + [VMEM] * (len(middle) + len(last) + 2),
        out_specs=[VMEM] * 3,
        scratch_shapes=[
            pltpu.VMEM(((blks - 1) * tiles_dev, tile_rows, row_width), jnp.bfloat16)
        ],
        compiler_params=LIMIT,
        cost_estimate=cost_of(capacity // 2, tile_rows, row_width),
    )(order, *middle, *last, blocks, total)
    summed = own
    for at, hop in enumerate(mine_chunks):
        pair = (mine[at] + far_arrived[at].astype(jnp.float32)).astype(jnp.bfloat16)
        near, pair = lax.optimization_barrier((near, pair))
        summed = summed + paired(pair, "grp", hop).astype(jnp.float32)
    summed = summed + paired(near, "grp", 1).astype(jnp.float32)
    inverse = lax.rsqrt(degrees.astype(jnp.float32))
    return (summed.reshape(1, row_count, row_width) * inverse[..., None]).astype(jnp.bfloat16)


def solution(mesh):
    placed = (
        P("side", ("grp", "blk"), None),
        P("side", ("grp", "blk")),
        P("side", ("grp", "blk")),
        P("side", ("grp", "blk"), None, None),
        P("side", None, ("grp", "blk")),
    )
    return jax.shard_map(
        shards,
        mesh=mesh,
        in_specs=placed,
        out_specs=P("side", ("grp", "blk"), None),
        check_vma=False,
    )
```

profile of v0, /device:TPU:0, one launch (start us, length us, event | category | flops | bytes accessed | tf_op | source)
XLA Modules:
  0.0 31.3 jit_solution(18253649609285133937)
XLA Ops:
  0.0 1.0 %shard_map.55 = bf16[4,128,128]{2,1,0:T(8,128)(2,1)S(1)} custom-call(s32[1,4]{1,0:T(1,128)} %exps_hbm.1, s32[1,512]{1,0:T(1,128)} %degrees_hbm.1, bf16[4,128,128]{2,1,0:T(8,128)(2,1)} %bitcast.15), custom_call_target="tpu_custom_call" | custom-call | flops 65536 | bytes 262144 | tf_op jit(solution)/shard_map/pallas_call | solution.py:51
  1.0 4.0 %collective-permute-start = (bf16[4,128,128]{2,1,0:T(8,128)(2,1)S(1)}, bf16[4,128,128]{2,1,0:T(8,128)(2,1)S(1)}, u32[]{:S(2)}, u32[]{:S(2)}) collective-permute-start(bf16[4,128,128]{2,1,0:T(8,128)(2,1)S(1)} %shard_map.55), channel_id=1, source_target_pairs={{0,18},{1,19},{2,16},{3,17},{16,2},{17,3},{18,0},{19,1},{4,22},{5,... | collective-permute-start | bytes 393224 | tf_op jit(solution)/shard_map/ppermute | solution.py:218
  4.9 0.5 %collective-permute-start.1 = (bf16[4,128,128]{2,1,0:T(8,128)(2,1)S(1)}, bf16[4,128,128]{2,1,0:T(8,128)(2,1)S(1)}, u32[]{:S(2)}, u32[]{:S(2)}) collective-permute-start(bf16[4,128,128]{2,1,0:T(8,128)(2,1)S(1)} %shard_map.55), channel_id=1, source_target_pairs={{0,16},{1,17},{2,18},{3,19},{16,0},{17,1},{18,2},{19,3},{4,20},{5,... | collective-permute-start | bytes 393224 | tf_op jit(solution)/shard_map/ppermute | solution.py:218
  5.5 0.1 pad_add_fusion.place_ref
  5.5 4.1 %shard_map.56 = (s32[5,112]{1,0:T(8,128)S(1)}, bf16[96,128,128]{2,1,0:T(8,128)(2,1)S(1)}) custom-call(s32[2]{0:T(128)S(1)} %pad_add_fusion.place_ref, s32[2,96]{1,0:T(2,128)} %bitcast.17, bf16[96,128,128]{2,1,0:T(8,128)(2,1)} %bitcast.13), custom_call_target="tpu_custom_call" | custom-call | tf_op jit(solution)/shard_map/pallas_call | solution.py:128
  9.7 0.0 collective-permute-done.panel
  9.7 0.1 collective-permute-start.2
  9.7 1.6 %shard_map.57.refs_3_ = f32[17,128,128]{2,1,0:T(8,128)S(1)} custom-call(s32[5,112]{1,0:T(8,128)S(1)} %get-tuple-element.21.order_ref, bf16[4,128,128]{2,1,0:T(8,128)(2,1)S(1)} %collective-permute-done.panel, bf16[96,128,128]{2,1,0:T(8,128)(2,1)S(1)} %get-tuple-element.23.blocks.refs_2_.refs_1_.refs_3_), custom_call_target="tpu_custom_call" | custom-call | flops 100663296 | bytes 786432 | tf_op jit(solution)/shard_map/pallas_call | solution.py:228
  11.4 0.1 collective-permute-done.1.refs_0_
  11.5 0.0 collective-permute-start.3
  11.5 0.0 collective-permute-done.2.refs_1_
  11.5 0.9 %shard_map.58.refs_2_ = f32[17,128,128]{2,1,0:T(8,128)S(1)} custom-call(s32[5,112]{1,0:T(8,128)S(1)} %get-tuple-element.21.order_ref, bf16[4,128,128]{2,1,0:T(8,128)(2,1)S(1)} %collective-permute-done.1.refs_0_, bf16[4,128,128]{2,1,0:T(8,128)(2,1)S(1)} %collective-permute-done.2.refs_1_, ...), custom_call_target="tpu_custom_call", output_to_operand_aliasing={{}: (4, {})} | custom-call | flops 100663296 | bytes 786432 | tf_op jit(solution)/shard_map/pallas_call | solution.py:240
  12.4 0.5 %collective-permute-done.3.refs_0_.refs_2_ = bf16[4,128,128]{2,1,0:T(8,128)(2,1)S(1)} collective-permute-done((bf16[4,128,128]{2,1,0:T(8,128)(2,1)S(1)}, bf16[4,128,128]{2,1,0:T(8,128)(2,1)S(1)}, u32[]{:S(2)}, u32[]{:S(2)}) %collective-permute-start.3) | collective-permute-done | bytes 131104 | tf_op jit(solution)/shard_map/ppermute | solution.py:221
  12.8 0.6 %shard_map.59 = (bf16[1,4,128,128]{3,2,1,0:T(8,128)(2,1)S(1)}, f32[17,128,128]{2,1,0:T(8,128)S(1)}) custom-call(s32[5,112]{1,0:T(8,128)S(1)} %get-tuple-element.21.order_ref, bf16[4,128,128]{2,1,0:T(8,128)(2,1)S(1)} %collective-permute-done.3.refs_0_.refs_2_, ...), custom_call_target="tpu_custom_call", output_to_operand_aliasing={{1}: (3, {})} | custom-call | flops 50331648 | bytes 393216 | tf_op jit(solution)/shard_map/pallas_call | solution.py:254
  13.5 1.6 %collective-permute-start.4 = (bf16[1,4,128,128]{3,2,1,0:T(8,128)(2,1)S(1)}, bf16[1,4,128,128]{3,2,1,0:T(8,128)(2,1)S(1)}, u32[]{:S(2)}, u32[]{:S(2)}) collective-permute-start(bf16[1,4,128,128]{3,2,1,0:T(8,128)(2,1)S(1)} %get-tuple-element.32), channel_id=1, source_target_pairs={{0,4},{4,0},{8,12},{12,8},{1,5},{5,1},{9,13},{13,9},{2,6},{6,2},{1... | collective-permute-start | bytes 393224 | tf_op jit(solution)/shard_map/ppermute | solution.py:221
  15.1 0.0 copy-start
  15.1 1.4 %shard_map.60 = (f32[4,128,128]{2,1,0:T(8,128)S(1)}, bf16[4,128,128]{2,1,0:T(8,128)(2,1)S(1)}, f32[1,4,128,128]{3,2,1,0:T(8,128)S(1)}) custom-call(s32[5,112]{1,0:T(8,128)S(1)} %get-tuple-element.21.order_ref, bf16[4,128,128]{2,1,0:T(8,128)(2,1)S(1)} %collective-permute-done.1.refs_0_, bf16[4,128,128]{2,1,0:T(8,128)(2,1)S(1)} %collective-permute-done.2.refs_1_, ...), custom_call_target="tpu_custom_call" | custom-call | flops 201326592 | bytes 1572864 | tf_op jit(solution)/shard_map/pallas_call | solution.py:271
  16.5 2.9 %collective-permute-done.4 = bf16[1,4,128,128]{3,2,1,0:T(8,128)(2,1)S(1)} collective-permute-done((bf16[1,4,128,128]{3,2,1,0:T(8,128)(2,1)S(1)}, bf16[1,4,128,128]{3,2,1,0:T(8,128)(2,1)S(1)}, u32[]{:S(2)}, u32[]{:S(2)}) %collective-permute-start.4) | collective-permute-done | bytes 131104 | tf_op jit(solution)/shard_map/ppermute | solution.py:221
  19.5 3.8 %collective-permute-start.5 = (bf16[4,128,128]{2,1,0:T(8,128)(2,1)S(1)}, bf16[4,128,128]{2,1,0:T(8,128)(2,1)S(1)}, u32[]{:S(2)}, u32[]{:S(2)}) collective-permute-start(bf16[4,128,128]{2,1,0:T(8,128)(2,1)S(1)} %fusion.1), channel_id=1, source_target_pairs={{0,8},{4,12},{8,0},{12,4},{1,9},{5,13},{9,1},{13,5},{2,10},{6,14},... | collective-permute-start | bytes 393224 | tf_op jit(solution)/shard_map/ppermute | solution.py:221
  23.3 0.3 collective-permute-start.6
  23.6 0.0 copy-done
  23.6 5.4 %collective-permute-done.5 = bf16[4,128,128]{2,1,0:T(8,128)(2,1)S(1)} collective-permute-done((bf16[4,128,128]{2,1,0:T(8,128)(2,1)S(1)}, bf16[4,128,128]{2,1,0:T(8,128)(2,1)S(1)}, u32[]{:S(2)}, u32[]{:S(2)}) %collective-permute-start.5) | collective-permute-done | bytes 131104 | tf_op jit(solution)/shard_map/ppermute | solution.py:221
  29.0 1.5 %collective-permute-done.6 = bf16[4,128,128]{2,1,0:T(8,128)(2,1)S(1)} collective-permute-done((bf16[4,128,128]{2,1,0:T(8,128)(2,1)S(1)}, bf16[4,128,128]{2,1,0:T(8,128)(2,1)S(1)}, u32[]{:S(2)}, u32[]{:S(2)}) %collective-permute-start.6) | collective-permute-done | bytes 131104 | tf_op jit(solution)/shard_map/ppermute | solution.py:221
  30.5 0.8 %fusion = bf16[1,512,128]{2,1,0:T(8,128)(2,1)} fusion(f32[512]{0:T(512)S(1)} %bitcast.16, f32[1,512,128]{2,1,0:T(8,128)S(1)} %bitcast.14), kind=kLoop, calls=%fused_computation.1 | loop fusion | flops 131072 | bytes 395264 | tf_op jit(solution)/shard_map/convert_element_type | solution.py:293
  (3 shorter events, 0.1 us)
Async XLA Ops:
  1.0 8.7 %collective-permute-start = (bf16[4,128,128]{2,1,0:T(8,128)(2,1)S(1)}, bf16[4,128,128]{2,1,0:T(8,128)(2,1)S(1)}, u32[]{:S(2)}, u32[]{:S(2)}) collective-permute-start(bf16[4,128,128]{2,1,0:T(8,128)(2,1)S(1)} %shard_map.55), channel_id=1, source_target_pairs={{0,18},{1,19},{2,16},{3,17},{16,2},{17,3},{18,0},{19,1},{4,22},{5,... | collective-permute-start | bytes 393224 | tf_op jit(solution)/shard_map/ppermute | solution.py:218
  4.9 6.6 %collective-permute-start.1 = (bf16[4,128,128]{2,1,0:T(8,128)(2,1)S(1)}, bf16[4,128,128]{2,1,0:T(8,128)(2,1)S(1)}, u32[]{:S(2)}, u32[]{:S(2)}) collective-permute-start(bf16[4,128,128]{2,1,0:T(8,128)(2,1)S(1)} %shard_map.55), channel_id=1, source_target_pairs={{0,16},{1,17},{2,18},{3,19},{16,0},{17,1},{18,2},{19,3},{4,20},{5,... | collective-permute-start | bytes 393224 | tf_op jit(solution)/shard_map/ppermute | solution.py:218
  9.7 1.8 %collective-permute-start.2 = (bf16[4,128,128]{2,1,0:T(8,128)(2,1)S(1)}, bf16[4,128,128]{2,1,0:T(8,128)(2,1)S(1)}, u32[]{:S(2)}, u32[]{:S(2)}) collective-permute-start(bf16[4,128,128]{2,1,0:T(8,128)(2,1)S(1)} %collective-permute-done.panel), channel_id=1, source_target_pairs={{0,1},{1,0},{2,3},{3,2},{4,5},{5,4},{6,7},{7,6},{8,9},{9,8},{10,11... | collective-permute-start | bytes 393224 | tf_op jit(solution)/shard_map/ppermute | solution.py:221
  11.5 1.3 %collective-permute-start.3 = (bf16[4,128,128]{2,1,0:T(8,128)(2,1)S(1)}, bf16[4,128,128]{2,1,0:T(8,128)(2,1)S(1)}, u32[]{:S(2)}, u32[]{:S(2)}) collective-permute-start(bf16[4,128,128]{2,1,0:T(8,128)(2,1)S(1)} %collective-permute-done.1.refs_0_), channel_id=1, source_target_pairs={{0,1},{1,0},{2,3},{3,2},{4,5},{5,4},{6,7},{7,6},{8,9},{9,8},{10,11... | collective-permute-start | bytes 393224 | tf_op jit(solution)/shard_map/ppermute | solution.py:221
  13.5 6.0 %collective-permute-start.4 = (bf16[1,4,128,128]{3,2,1,0:T(8,128)(2,1)S(1)}, bf16[1,4,128,128]{3,2,1,0:T(8,128)(2,1)S(1)}, u32[]{:S(2)}, u32[]{:S(2)}) collective-permute-start(bf16[1,4,128,128]{3,2,1,0:T(8,128)(2,1)S(1)} %get-tuple-element.32), channel_id=1, source_target_pairs={{0,4},{4,0},{8,12},{12,8},{1,5},{5,1},{9,13},{13,9},{2,6},{6,2},{1... | collective-permute-start | bytes 393224 | tf_op jit(solution)/shard_map/ppermute | solution.py:221
  15.1 8.5 %copy-start = (s32[1,512]{1,0:T(1,128)S(1)}, s32[1,512]{1,0:T(1,128)}, u32[]{:S(2)}) copy-start(s32[1,512]{1,0:T(1,128)} %degrees_hbm.1) | copy-start | bytes 6148
  19.5 9.5 %collective-permute-start.5 = (bf16[4,128,128]{2,1,0:T(8,128)(2,1)S(1)}, bf16[4,128,128]{2,1,0:T(8,128)(2,1)S(1)}, u32[]{:S(2)}, u32[]{:S(2)}) collective-permute-start(bf16[4,128,128]{2,1,0:T(8,128)(2,1)S(1)} %fusion.1), channel_id=1, source_target_pairs={{0,8},{4,12},{8,0},{12,4},{1,9},{5,13},{9,1},{13,5},{2,10},{6,14},... | collective-permute-start | bytes 393224 | tf_op jit(solution)/shard_map/ppermute | solution.py:221
  23.3 7.1 %collective-permute-start.6 = (bf16[4,128,128]{2,1,0:T(8,128)(2,1)S(1)}, bf16[4,128,128]{2,1,0:T(8,128)(2,1)S(1)}, u32[]{:S(2)}, u32[]{:S(2)}) collective-permute-start(bf16[4,128,128]{2,1,0:T(8,128)(2,1)S(1)} %get-tuple-element.34), channel_id=1, source_target_pairs={{0,4},{4,0},{8,12},{12,8},{1,5},{5,1},{9,13},{13,9},{2,6},{6,2},{1... | collective-permute-start | bytes 393224 | tf_op jit(solution)/shard_map/ppermute | solution.py:221
where the time goes:
time: 31.4 us; the launch traced here: 31.3 us
  waiting for transfers between devices  10.4 us (33%)
  starting transfers between devices  10.3 us (33%)
  Pallas kernels  9.58 us (31%)
  other arithmetic  0.95 us (3%)
    ppermute x5, waiting for transfers between devices, paired(): lax.ppermute(value, axis, [(at, at ^ hop) for at in range(lax.axis_size(a...  10.3 us
    ppermute x5, starting transfers between devices, paired(): lax.ppermute(value, axis, [(at, at ^ hop) for at in range(lax.axis_size(a...  5.85 us
    ppermute x2, starting transfers between devices, across(): return lax.ppermute(value, ('side', 'blk'), pairs)  4.49 us
    pallas_call x1, Pallas kernels, stage_blocks(): pl.pallas_call(functools.partial(stage_kernel, blks, groups, tiles_dev),...  4.1 us
    pallas_call x1, Pallas kernels, shards(): pl.pallas_call(first_kernel, out_shape=total_shape, in_specs=[SMEM] + [VM...  1.64 us
    pallas_call x1, Pallas kernels, shards(): pl.pallas_call(functools.partial(near_kernel, tiles_dev, mine_chunks), ou...  1.39 us
    pallas_call x1, Pallas kernels, scale_rows(): pl.pallas_call(scale_kernel, out_shape=jax.ShapeDtypeStruct(codes.shape,...  0.97 us
    pallas_call x1, Pallas kernels, shards(): pl.pallas_call(second_kernel, out_shape=total_shape, in_specs=[SMEM] + [V...  0.85 us
  transfers between devices with their start and end apart: 7, of which 5 were waited for; matrix products, arithmetic and copies ran while one was open for 0% of the time, Pallas kernels for 26%

commit v1 on v0

--- a/solution.py
+++ b/solution.py
@@ -8,7 +8,7 @@
 from jax.sharding import PartitionSpec as P
 
 UNROLL = 8
-STAGES = 4
+STAGES = 3
 VMEM = pl.BlockSpec(memory_space=pltpu.VMEM)
 SMEM = pl.BlockSpec(memory_space=pltpu.SMEM)
 HBM = pl.BlockSpec(memory_space=pltpu.HBM)
@@ -90,13 +90,11 @@
         rank = half - 1 - (hop >> 1)
         odd = hop & 1
         far = (chunk >= 2) & ((chunk & 1) == 1)
-        first = (odd == 0) & (rank == 0)
-        last = (odd == 1) & (rank > 0)
-        stage = jnp.where(first, 0, jnp.where(far, jnp.where(last, 2, 1), 3))
+        stage = jnp.where(far, jnp.minimum(rank + odd, 1), 2)
         stage = jnp.where(origin < source_tiles, stage, STAGES)
-        panel = jnp.where(odd == 1, jnp.where(rank == 0, half - 1, rank - 1), rank - 1)
-        panel = jnp.where(last & (stage == 3), panel + half, jnp.maximum(panel, 0))
-        word = pack(slot, panel * tiles_dev + row, chunk * tiles_dev + tile)
+        panel = rank + odd * half - (stage == 1).astype(jnp.int32)
+        kept = jnp.where(far, (chunk - 3) >> 1, chunk)
+        word = pack(slot, panel * tiles_dev + row, kept * tiles_dev + tile)
         where = jnp.int32(0)
         for at, position in enumerate(nexts):
             where = jnp.where(stage == at, position, where)
@@ -106,8 +104,9 @@
         )
 
     ends = lax.fori_loop(0, capacity, enlist, (jnp.int32(0),) * STAGES, unroll=8)
-    spare = pack(0, 0, groups * tiles_dev)
-    for at, end in enumerate(ends):
+    far_tiles = (groups // 2 - 1) * tiles_dev
+    spares = [pack(0, 0, far_tiles)] * 2 + [pack(0, 0, groups * tiles_dev)]
+    for at, (end, spare) in enumerate(zip(ends, spares)):
         for extra in range(UNROLL):
             order_ref[at, end + extra] = spare
         order_ref[at, capacity + UNROLL] = split(end + (UNROLL - 1), UNROLL)[0]
@@ -160,29 +159,23 @@
         source[at * rows : (at + 1) * rows] = panel[...]
 
 
-def first_kernel(order_ref, panel, blocks, total):
+def early_kernel(order_ref, panel, blocks, total):
     total[...] = jnp.zeros_like(total)
     add_products(0, order_ref, blocks, panel, total)
 
 
-def second_kernel(order_ref, *refs):
-    *panels, blocks, _, total, source = refs
+def far_kernel(order_ref, *refs):
+    *panels, blocks, total, far, source = refs
     gather_panels(panels, source)
     add_products(1, order_ref, blocks, source, total)
-
-
-def far_kernel(tiles_dev, chunks, order_ref, *refs):
-    *panels, blocks, _, far, total, source = refs
+    far[...] = total[: far.shape[0]].astype(far.dtype)
+
+
+def rest_kernel(tiles_dev, chunks, order_ref, *refs):
+    *panels, blocks, own, near, mine, source, total = refs
     gather_panels(panels, source)
+    total[...] = jnp.zeros_like(total)
     add_products(2, order_ref, blocks, source, total)
-    for at, chunk in enumerate(chunks):
-        far[at] = total[chunk * tiles_dev : (chunk + 1) * tiles_dev].astype(far.dtype)
-
-
-def near_kernel(tiles_dev, chunks, order_ref, *refs):
-    *panels, blocks, total, own, near, mine, source = refs
-    gather_panels(panels, source)
-    add_products(3, order_ref, blocks, source, total)
     own[...] = total[:tiles_dev]
     near[...] = total[tiles_dev : 2 * tiles_dev].astype(near.dtype)
     for at, chunk in enumerate(chunks):
@@ -224,65 +217,51 @@
     early, *middle = [across(source, hop) for hop in reversed(range(0, blks, 2))]
     order, blocks = stage_blocks(block_index[0], place, adjacency[0], blks, groups, tiles_dev)
     early, order = lax.optimization_barrier((early, order))
-    total_shape = jax.ShapeDtypeStruct((dest_tiles + 1, tile_rows, row_width), jnp.float32)
+    other = paired(early, "blk", 1)
+    far_chunks, mine_chunks = range(3, groups, 2), range(2, groups, 2)
+    far_tiles = len(far_chunks) * tiles_dev
+
+    def held(count, dtype):
+        return pltpu.VMEM((count, tile_rows, row_width), dtype)
+
     total = pl.pallas_call(
-        first_kernel,
-        out_shape=total_shape,
+        early_kernel,
+        out_shape=jax.ShapeDtypeStruct((far_tiles + 1, tile_rows, row_width), jnp.float32),
         in_specs=[SMEM] + [VMEM] * 2,
         out_specs=VMEM,
         compiler_params=LIMIT,
-        cost_estimate=cost_of(capacity // 4, tile_rows, row_width),
+        cost_estimate=cost_of(capacity // 8, tile_rows, row_width),
     )(order, early, blocks)
-    other = paired(early, "blk", 1)
     *middle, total = lax.optimization_barrier((*middle, total))
-    last = [paired(panel, "blk", 1) for panel in middle]
-    middle += [other]
-    total = pl.pallas_call(
-        second_kernel,
-        out_shape=total_shape,
-        in_specs=[SMEM] + [VMEM] * (len(middle) + 2),
+    panels = middle + [other] + [paired(panel, "blk", 1) for panel in middle]
+    far = pl.pallas_call(
+        far_kernel,
+        out_shape=jax.ShapeDtypeStruct((far_tiles, tile_rows, row_width), jnp.bfloat16),
+        in_specs=[SMEM] + [VMEM] * (len(panels) + 2),
         out_specs=VMEM,
-        input_output_aliases={len(middle) + 2: 0},
-        scratch_shapes=[
-            pltpu.VMEM((len(middle) * tiles_dev, tile_rows, row_width), jnp.bfloat16)
-        ],
-        compiler_params=LIMIT,
-        cost_estimate=cost_of(capacity // 4, tile_rows, row_width),
-    )(order, *middle, blocks, total)
-    *last, total = lax.optimization_barrier((*last, total))
-    far_chunks = range(3, groups, 2)
-    far, total = pl.pallas_call(
-        functools.partial(far_kernel, tiles_dev, far_chunks),
-        out_shape=[
-            jax.ShapeDtypeStruct((len(far_chunks),) + part, jnp.bfloat16),
-            total_shape,
-        ],
-        in_specs=[SMEM] + [VMEM] * (len(last) + 2),
-        out_specs=[VMEM, VMEM],
-        input_output_aliases={len(last) + 2: 1},
-        scratch_shapes=[
-            pltpu.VMEM((len(last) * tiles_dev, tile_rows, row_width), jnp.bfloat16)
-        ],
+        scratch_shapes=[held(len(panels) * tiles_dev, jnp.bfloat16)],
         compiler_params=LIMIT,
         cost_estimate=cost_of(capacity // 8, tile_rows, row_width),
-    )(order, *last, blocks, total)
-    far_arrived = paired(far, "grp", 1)
-    mine_chunks = range(2, groups, 2)
+    )(order, *panels, blocks, total)
+    far, order = lax.optimization_barrier((far, order))
+    far_arrived = paired(far, "grp", 1).reshape((len(far_chunks),) + part)
+    panels = [early] + panels
     own, near, mine = pl.pallas_call(
-        functools.partial(near_kernel, tiles_dev, mine_chunks),
+        functools.partial(rest_kernel, tiles_dev, mine_chunks),
         out_shape=[
             jax.ShapeDtypeStruct(part, jnp.float32),
             jax.ShapeDtypeStruct(part, jnp.bfloat16),
             jax.ShapeDtypeStruct((len(mine_chunks),) + part, jnp.float32),
         ],
-        in_specs=[SMEM] + [VMEM] * (len(middle) + len(last) + 2),
+        in_specs=[SMEM] + [VMEM] * (len(panels) + 1),
         out_specs=[VMEM] * 3,
         scratch_shapes=[
-            pltpu.VMEM(((blks - 1) * tiles_dev, tile_rows, row_width), jnp.bfloat16)
-        ],
-        compiler_params=LIMIT,
-        cost_estimate=cost_of(capacity // 2, tile_rows, row_width),
-    )(order, *middle, *last, blocks, total)
+            held(len(panels) * tiles_dev, jnp.bfloat16),
+            held(dest_tiles + 1, jnp.float32),
+        ],
+        compiler_params=LIMIT,
+        cost_estimate=cost_of(capacity, tile_rows, row_width),
+    )(order, *panels, blocks)
     summed = own
     for at, hop in enumerate(mine_chunks):
         pair = (mine[at] + far_arrived[at].astype(jnp.float32)).astype(jnp.bfloat16)

time: 31.4 us -> 30.2 us (0.962); the launches traced: 31.3 us -> 29.8 us
  Pallas kernels: 9.58 us -> 8.15 us
  waiting for transfers between devices: 10.4 us -> 9.99 us
    ppermute x5, waiting for transfers between devices: 10.3 us -> 8.27 us  [paired(): lax.ppermute(value, axis, [(at, at ^ hop) for at in range(lax.axis_size(a...]
    ppermute x2, waiting for transfers between devices: 0.11 us -> 1.72 us  [across(): return lax.ppermute(value, ('side', 'blk'), pairs)]
    pallas_call x4 -> x3, Pallas kernels: 4.51 us -> 3.57 us  [the longest x1 1.9 us: shards(): pl.pallas_call(functools.partial(rest_kernel, tiles_dev, mine_chunks), ou...]
    pallas_call x1, Pallas kernels: 4.1 us -> 3.61 us  [stage_blocks(): pl.pallas_call(functools.partial(stage_kernel, blks, groups, tiles_dev),...]
  transfers between devices with their start and end apart: 7 -> 7, of which waited for: 5 -> 7; matrix products, arithmetic and copies ran while one was open for 0% -> 0% of each run, Pallas kernels for 26% -> 20%
where the time goes in v1:
time: 30.2 us; the launch traced here: 29.8 us
  starting transfers between devices  10.6 us (35%)
  waiting for transfers between devices  9.99 us (33%)
  Pallas kernels  8.15 us (27%)
  other arithmetic  0.94 us (3%)
    ppermute x5, waiting for transfers between devices, paired(): lax.ppermute(value, axis, [(at, at ^ hop) for at in range(lax.axis_size(a...  8.27 us
    ppermute x5, starting transfers between devices, paired(): lax.ppermute(value, axis, [(at, at ^ hop) for at in range(lax.axis_size(a...  6.14 us
    ppermute x2, starting transfers between devices, across(): return lax.ppermute(value, ('side', 'blk'), pairs)  4.49 us
    pallas_call x1, Pallas kernels, stage_blocks(): pl.pallas_call(functools.partial(stage_kernel, blks, groups, tiles_dev),...  3.61 us
    pallas_call x1, Pallas kernels, shards(): pl.pallas_call(functools.partial(rest_kernel, tiles_dev, mine_chunks), ou...  1.9 us
    ppermute x2, waiting for transfers between devices, across(): return lax.ppermute(value, ('side', 'blk'), pairs)  1.72 us
    pallas_call x1, Pallas kernels, shards(): pl.pallas_call(far_kernel, out_shape=jax.ShapeDtypeStruct((far_tiles, til...  1.08 us
    pallas_call x1, Pallas kernels, scale_rows(): pl.pallas_call(scale_kernel, out_shape=jax.ShapeDtypeStruct(codes.shape,...  0.97 us
  transfers between devices with their start and end apart: 7, of which 7 were waited for; matrix products, arithmetic and copies ran while one was open for 0% of the time, Pallas kernels for 20%

profile of v1, /device:TPU:0, one launch (start us, length us, event | category | flops | bytes accessed | tf_op | source)
XLA Modules:
  0.0 29.8 jit_solution(8062325271049627053)
XLA Ops:
  0.0 1.0 %shard_map.55 = bf16[4,128,128]{2,1,0:T(8,128)(2,1)S(1)} custom-call(s32[1,4]{1,0:T(1,128)} %exps_hbm.1, s32[1,512]{1,0:T(1,128)} %degrees_hbm.1, bf16[4,128,128]{2,1,0:T(8,128)(2,1)} %bitcast.17), custom_call_target="tpu_custom_call" | custom-call | flops 65536 | bytes 262144 | tf_op jit(solution)/shard_map/pallas_call | solution.py:51
  1.0 4.0 %collective-permute-start = (bf16[4,128,128]{2,1,0:T(8,128)(2,1)S(1)}, bf16[4,128,128]{2,1,0:T(8,128)(2,1)S(1)}, u32[]{:S(2)}, u32[]{:S(2)}) collective-permute-start(bf16[4,128,128]{2,1,0:T(8,128)(2,1)S(1)} %shard_map.55), channel_id=1, source_target_pairs={{0,18},{1,19},{2,16},{3,17},{16,2},{17,3},{18,0},{19,1},{4,22},{5,... | collective-permute-start | bytes 393224 | tf_op jit(solution)/shard_map/ppermute | solution.py:211
  4.9 0.5 %collective-permute-start.1 = (bf16[4,128,128]{2,1,0:T(8,128)(2,1)S(1)}, bf16[4,128,128]{2,1,0:T(8,128)(2,1)S(1)}, u32[]{:S(2)}, u32[]{:S(2)}) collective-permute-start(bf16[4,128,128]{2,1,0:T(8,128)(2,1)S(1)} %shard_map.55), channel_id=1, source_target_pairs={{0,16},{1,17},{2,18},{3,19},{16,0},{17,1},{18,2},{19,3},{4,20},{5,... | collective-permute-start | bytes 393224 | tf_op jit(solution)/shard_map/ppermute | solution.py:211
  5.5 0.1 pad_add_fusion.place_ref
  5.5 3.6 %shard_map.56 = (s32[4,112]{1,0:T(4,128)S(1)}, bf16[96,128,128]{2,1,0:T(8,128)(2,1)S(1)}) custom-call(s32[2]{0:T(128)S(1)} %pad_add_fusion.place_ref, s32[2,96]{1,0:T(2,128)} %bitcast.19, bf16[96,128,128]{2,1,0:T(8,128)(2,1)} %bitcast.15), custom_call_target="tpu_custom_call" | custom-call | tf_op jit(solution)/shard_map/pallas_call | solution.py:127
  9.2 0.1 collective-permute-done.panel.refs_0_
  9.3 0.6 %shard_map.57.refs_4_ = f32[5,128,128]{2,1,0:T(8,128)S(1)} custom-call(s32[4,112]{1,0:T(4,128)S(1)} %get-tuple-element.24.order_ref, bf16[4,128,128]{2,1,0:T(8,128)(2,1)S(1)} %collective-permute-done.panel.refs_0_, bf16[96,128,128]{2,1,0:T(8,128)(2,1)S(1)} %get-tuple-element.21.blocks.refs_3_.refs_4_), custom_call_target="tpu_custom_call" | custom-call | flops 50331648 | bytes 393216 | tf_op jit(solution)/shard_map/pallas_call | solution.py:227
  9.9 0.0 copy-start
  9.9 1.6 %collective-permute-done.1.refs_0_.refs_1_ = bf16[4,128,128]{2,1,0:T(8,128)(2,1)S(1)} collective-permute-done((bf16[4,128,128]{2,1,0:T(8,128)(2,1)S(1)}, bf16[4,128,128]{2,1,0:T(8,128)(2,1)S(1)}, u32[]{:S(2)}, u32[]{:S(2)}) %collective-permute-start.1) | collective-permute-done | bytes 131104 | tf_op jit(solution)/shard_map/ppermute | solution.py:211
  11.5 0.0 collective-permute-start.3
  11.5 0.5 %collective-permute-start.2 = (bf16[4,128,128]{2,1,0:T(8,128)(2,1)S(1)}, bf16[4,128,128]{2,1,0:T(8,128)(2,1)S(1)}, u32[]{:S(2)}, u32[]{:S(2)}) collective-permute-start(bf16[4,128,128]{2,1,0:T(8,128)(2,1)S(1)} %collective-permute-done.panel.refs_0_), channel_id=1, source_target_pairs={{0,1},{1,0},{2,3},{3,2},{4,5},{5,4},{6,7},{7,6},{8,9},{9,8},{10,11... | collective-permute-start | bytes 393224 | tf_op jit(solution)/shard_map/ppermute | solution.py:214
  12.0 0.8 %collective-permute-done.3.refs_2_.refs_3_ = bf16[4,128,128]{2,1,0:T(8,128)(2,1)S(1)} collective-permute-done((bf16[4,128,128]{2,1,0:T(8,128)(2,1)S(1)}, bf16[4,128,128]{2,1,0:T(8,128)(2,1)S(1)}, u32[]{:S(2)}, u32[]{:S(2)}) %collective-permute-start.3) | collective-permute-done | bytes 131104 | tf_op jit(solution)/shard_map/ppermute | solution.py:214
  12.8 0.2 collective-permute-done.2.refs_1_.refs_2_
  13.0 1.1 %shard_map.58 = bf16[4,128,128]{2,1,0:T(8,128)(2,1)S(1)} custom-call(s32[4,112]{1,0:T(4,128)S(1)} %get-tuple-element.24.order_ref, bf16[4,128,128]{2,1,0:T(8,128)(2,1)S(1)} %collective-permute-done.1.refs_0_.refs_1_, bf16[4,128,128]{2,1,0:T(8,128)(2,1)S(1)} %collective-permute-done.2.refs_1_.refs_2_, ...), custom_call_target="tpu_custom_call" | custom-call | flops 50331648 | bytes 393216 | tf_op jit(solution)/shard_map/pallas_call | solution.py:237
  14.1 1.4 %collective-permute-start.4 = (bf16[4,128,128]{2,1,0:T(8,128)(2,1)S(1)}, bf16[4,128,128]{2,1,0:T(8,128)(2,1)S(1)}, u32[]{:S(2)}, u32[]{:S(2)}) collective-permute-start(bf16[4,128,128]{2,1,0:T(8,128)(2,1)S(1)} %shard_map.58), channel_id=1, source_target_pairs={{0,4},{4,0},{8,12},{12,8},{1,5},{5,1},{9,13},{13,9},{2,6},{6,2},{1... | collective-permute-start | bytes 393224 | tf_op jit(solution)/shard_map/ppermute | solution.py:214
  15.5 1.9 %shard_map.59 = (f32[4,128,128]{2,1,0:T(8,128)S(1)}, bf16[4,128,128]{2,1,0:T(8,128)(2,1)S(1)}, f32[1,4,128,128]{3,2,1,0:T(8,128)S(1)}) custom-call(s32[4,112]{1,0:T(4,128)S(1)} %get-tuple-element.24.order_ref, bf16[4,128,128]{2,1,0:T(8,128)(2,1)S(1)} %collective-permute-done.panel.refs_0_, bf16[4,128,128]{2,1,0:T(8,128)(2,1)S(1)} %collective-permute-done.1.refs_0_.refs_1_, ...), custom_call_target="tpu_custom_call" | custom-call | flops 402653184 | bytes 3145728 | tf_op jit(solution)/shard_map/pallas_call | solution.py:249
  17.4 2.5 %collective-permute-done.4 = bf16[4,128,128]{2,1,0:T(8,128)(2,1)S(1)} collective-permute-done((bf16[4,128,128]{2,1,0:T(8,128)(2,1)S(1)}, bf16[4,128,128]{2,1,0:T(8,128)(2,1)S(1)}, u32[]{:S(2)}, u32[]{:S(2)}) %collective-permute-start.4) | collective-permute-done | bytes 131104 | tf_op jit(solution)/shard_map/ppermute | solution.py:214
  19.9 2.7 %collective-permute-start.5 = (bf16[4,128,128]{2,1,0:T(8,128)(2,1)S(1)}, bf16[4,128,128]{2,1,0:T(8,128)(2,1)S(1)}, u32[]{:S(2)}, u32[]{:S(2)}) collective-permute-start(bf16[4,128,128]{2,1,0:T(8,128)(2,1)S(1)} %fusion.1), channel_id=1, source_target_pairs={{0,8},{4,12},{8,0},{12,4},{1,9},{5,13},{9,1},{13,5},{2,10},{6,14},... | collective-permute-start | bytes 393224 | tf_op jit(solution)/shard_map/ppermute | solution.py:214
  22.6 1.6 %collective-permute-start.6 = (bf16[4,128,128]{2,1,0:T(8,128)(2,1)S(1)}, bf16[4,128,128]{2,1,0:T(8,128)(2,1)S(1)}, u32[]{:S(2)}, u32[]{:S(2)}) collective-permute-start(bf16[4,128,128]{2,1,0:T(8,128)(2,1)S(1)} %get-tuple-element.30), channel_id=1, source_target_pairs={{0,4},{4,0},{8,12},{12,8},{1,5},{5,1},{9,13},{13,9},{2,6},{6,2},{1... | collective-permute-start | bytes 393224 | tf_op jit(solution)/shard_map/ppermute | solution.py:214
  24.2 0.0 copy-done
  24.2 4.5 %collective-permute-done.5 = bf16[4,128,128]{2,1,0:T(8,128)(2,1)S(1)} collective-permute-done((bf16[4,128,128]{2,1,0:T(8,128)(2,1)S(1)}, bf16[4,128,128]{2,1,0:T(8,128)(2,1)S(1)}, u32[]{:S(2)}, u32[]{:S(2)}) %collective-permute-start.5) | collective-permute-done | bytes 131104 | tf_op jit(solution)/shard_map/ppermute | solution.py:214
  28.7 0.2 collective-permute-done.6
  29.0 0.8 %fusion = bf16[1,512,128]{2,1,0:T(8,128)(2,1)} fusion(f32[512]{0:T(512)S(1)} %bitcast.18, f32[1,512,128]{2,1,0:T(8,128)S(1)} %bitcast.16), kind=kLoop, calls=%fused_computation.1 | loop fusion | flops 131072 | bytes 395264 | tf_op jit(solution)/shard_map/convert_element_type | solution.py:272
  (3 shorter events, 0.1 us)
Async XLA Ops:
  1.0 8.3 %collective-permute-start = (bf16[4,128,128]{2,1,0:T(8,128)(2,1)S(1)}, bf16[4,128,128]{2,1,0:T(8,128)(2,1)S(1)}, u32[]{:S(2)}, u32[]{:S(2)}) collective-permute-start(bf16[4,128,128]{2,1,0:T(8,128)(2,1)S(1)} %shard_map.55), channel_id=1, source_target_pairs={{0,18},{1,19},{2,16},{3,17},{16,2},{17,3},{18,0},{19,1},{4,22},{5,... | collective-permute-start | bytes 393224 | tf_op jit(solution)/shard_map/ppermute | solution.py:211
  4.9 6.6 %collective-permute-start.1 = (bf16[4,128,128]{2,1,0:T(8,128)(2,1)S(1)}, bf16[4,128,128]{2,1,0:T(8,128)(2,1)S(1)}, u32[]{:S(2)}, u32[]{:S(2)}) collective-permute-start(bf16[4,128,128]{2,1,0:T(8,128)(2,1)S(1)} %shard_map.55), channel_id=1, source_target_pairs={{0,16},{1,17},{2,18},{3,19},{16,0},{17,1},{18,2},{19,3},{4,20},{5,... | collective-permute-start | bytes 393224 | tf_op jit(solution)/shard_map/ppermute | solution.py:211
  9.9 14.3 %copy-start = (s32[1,512]{1,0:T(1,128)S(1)}, s32[1,512]{1,0:T(1,128)}, u32[]{:S(2)}) copy-start(s32[1,512]{1,0:T(1,128)} %degrees_hbm.1) | copy-start | bytes 6148
  11.5 1.3 %collective-permute-start.3 = (bf16[4,128,128]{2,1,0:T(8,128)(2,1)S(1)}, bf16[4,128,128]{2,1,0:T(8,128)(2,1)S(1)}, u32[]{:S(2)}, u32[]{:S(2)}) collective-permute-start(bf16[4,128,128]{2,1,0:T(8,128)(2,1)S(1)} %collective-permute-done.1.refs_0_.refs_1_), channel_id=1, source_target_pairs={{0,1},{1,0},{2,3},{3,2},{4,5},{5,4},{6,7},{7,6},{8,9},{9,8},{10,11... | collective-permute-start | bytes 393224 | tf_op jit(solution)/shard_map/ppermute | solution.py:214
  11.5 1.5 %collective-permute-start.2 = (bf16[4,128,128]{2,1,0:T(8,128)(2,1)S(1)}, bf16[4,128,128]{2,1,0:T(8,128)(2,1)S(1)}, u32[]{:S(2)}, u32[]{:S(2)}) collective-permute-start(bf16[4,128,128]{2,1,0:T(8,128)(2,1)S(1)} %collective-permute-done.panel.refs_0_), channel_id=1, source_target_pairs={{0,1},{1,0},{2,3},{3,2},{4,5},{5,4},{6,7},{7,6},{8,9},{9,8},{10,11... | collective-permute-start | bytes 393224 | tf_op jit(solution)/shard_map/ppermute | solution.py:214
  14.1 5.8 %collective-permute-start.4 = (bf16[4,128,128]{2,1,0:T(8,128)(2,1)S(1)}, bf16[4,128,128]{2,1,0:T(8,128)(2,1)S(1)}, u32[]{:S(2)}, u32[]{:S(2)}) collective-permute-start(bf16[4,128,128]{2,1,0:T(8,128)(2,1)S(1)} %shard_map.58), channel_id=1, source_target_pairs={{0,4},{4,0},{8,12},{12,8},{1,5},{5,1},{9,13},{13,9},{2,6},{6,2},{1... | collective-permute-start | bytes 393224 | tf_op jit(solution)/shard_map/ppermute | solution.py:214
  19.9 8.8 %collective-permute-start.5 = (bf16[4,128,128]{2,1,0:T(8,128)(2,1)S(1)}, bf16[4,128,128]{2,1,0:T(8,128)(2,1)S(1)}, u32[]{:S(2)}, u32[]{:S(2)}) collective-permute-start(bf16[4,128,128]{2,1,0:T(8,128)(2,1)S(1)} %fusion.1), channel_id=1, source_target_pairs={{0,8},{4,12},{8,0},{12,4},{1,9},{5,13},{9,1},{13,5},{2,10},{6,14},... | collective-permute-start | bytes 393224 | tf_op jit(solution)/shard_map/ppermute | solution.py:214
  22.6 6.4 %collective-permute-start.6 = (bf16[4,128,128]{2,1,0:T(8,128)(2,1)S(1)}, bf16[4,128,128]{2,1,0:T(8,128)(2,1)S(1)}, u32[]{:S(2)}, u32[]{:S(2)}) collective-permute-start(bf16[4,128,128]{2,1,0:T(8,128)(2,1)S(1)} %get-tuple-element.30), channel_id=1, source_target_pairs={{0,4},{4,0},{8,12},{12,8},{1,5},{5,1},{9,13},{13,9},{2,6},{6,2},{1... | collective-permute-start | bytes 393224 | tf_op jit(solution)/shard_map/ppermute | solution.py:214

commit v2 on v1

--- a/solution.py
+++ b/solution.py
@@ -25,7 +25,7 @@
     return value // size, value % size
 
 
-def scale_kernel(exps_hbm, degrees_hbm, codes_hbm, rows, exps_ref, degrees, codes, sems):
+def scale_kernel(exps_hbm, degrees_hbm, codes_hbm, rows, factors, exps_ref, degrees, codes, sems):
     pairs = [(exps_hbm, exps_ref), (degrees_hbm, degrees), (codes_hbm, codes)]
     fetches = [
         pltpu.make_async_copy(held, wanted, sems.at[at])
@@ -37,22 +37,25 @@
     fetches[1].wait()
     tiles_dev, tile_rows, row_width = rows.shape
     inverse = lax.rsqrt(degrees[...].astype(jnp.float32))
-    factors = []
     for tile in range(tiles_dev):
         lanes = inverse[:, tile * tile_rows : (tile + 1) * tile_rows]
-        scale = jnp.exp2(jnp.full(lanes.shape, exps_ref[0, tile], jnp.int32).astype(jnp.float32))
-        factors.append(jnp.broadcast_to(lanes * scale, (row_width, tile_rows)).T)
+        factors[tile] = jnp.broadcast_to(lanes, (row_width, tile_rows)).T
     fetches[2].wait()
-    for tile, factor in enumerate(factors):
-        rows[tile] = (codes[tile].astype(jnp.float32) * factor).astype(rows.dtype)
+    for tile in range(tiles_dev):
+        scale = jnp.exp2(jnp.full((1, 1), exps_ref[0, tile], jnp.int32).astype(jnp.float32))
+        scaled = codes[tile].astype(jnp.float32) * scale * factors[tile]
+        rows[tile] = scaled.astype(rows.dtype)
 
 
 def scale_rows(codes, exps, degrees):
     return pl.pallas_call(
         scale_kernel,
-        out_shape=jax.ShapeDtypeStruct(codes.shape, jnp.bfloat16),
+        out_shape=[
+            jax.ShapeDtypeStruct(codes.shape, jnp.bfloat16),
+            jax.ShapeDtypeStruct(codes.shape, jnp.float32),
+        ],
         in_specs=[HBM] * 3,
-        out_specs=VMEM,
+        out_specs=[VMEM] * 2,
         scratch_shapes=[
             pltpu.SMEM(exps.shape, exps.dtype),
             pltpu.VMEM(degrees.shape, degrees.dtype),
@@ -164,22 +167,47 @@
     add_products(0, order_ref, blocks, panel, total)
 
 
-def far_kernel(order_ref, *refs):
-    *panels, blocks, total, far, source = refs
+def far_kernel(half, order_ref, *refs):
+    *panels, blocks, total, far, straight, source = refs
     gather_panels(panels, source)
     add_products(1, order_ref, blocks, source, total)
-    far[...] = total[: far.shape[0]].astype(far.dtype)
-
-
-def rest_kernel(tiles_dev, chunks, order_ref, *refs):
-    *panels, blocks, own, near, mine, source, total = refs
+    tiles_dev = half + straight.shape[1]
+    for at in range(far.shape[0]):
+        chunk = total.at[pl.ds(at * tiles_dev, tiles_dev)]
+        far[at] = chunk[:half].astype(far.dtype)
+        straight[at] = chunk[half:].astype(straight.dtype)
+
+
+def rest_kernel(half, chunks, order_ref, *refs):
+    *panels, blocks, own_low, own_high, near, mine, straight, source, total = refs
     gather_panels(panels, source)
     total[...] = jnp.zeros_like(total)
     add_products(2, order_ref, blocks, source, total)
-    own[...] = total[:tiles_dev]
+    tiles_dev = near.shape[0]
+    own_low[...] = total[:half]
+    own_high[...] = total[half:tiles_dev]
     near[...] = total[tiles_dev : 2 * tiles_dev].astype(near.dtype)
     for at, chunk in enumerate(chunks):
-        mine[at] = total[chunk * tiles_dev : (chunk + 1) * tiles_dev]
+        begin = chunk * tiles_dev
+        mine[at] = total[begin : begin + half]
+        straight[at] = total[begin + half : begin + tiles_dev].astype(straight.dtype)
+
+
+def final_kernel(factors, near, own_low, own_high, *refs):
+    *arrived, out_hbm, out, sems = refs
+    half = own_low.shape[0]
+    lows, highs = arrived[: len(arrived) // 2], arrived[len(arrived) // 2 :]
+    copies = []
+    for tile in range(out.shape[0]):
+        own, pieces, at = (own_low, lows, tile) if tile < half else (own_high, highs, tile - half)
+        value = own[at] + near[tile].astype(jnp.float32)
+        for piece in pieces:
+            value = value + piece[at].astype(jnp.float32)
+        out[tile] = (value * factors[tile]).astype(out.dtype)
+        copies.append(pltpu.make_async_copy(out.at[tile], out_hbm.at[tile], sems.at[tile]))
+        copies[-1].start()
+    for copy in copies:
+        copy.wait()
 
 
 def cost_of(slots, tile_rows, row_width):
@@ -200,7 +228,7 @@
     blks = lax.axis_size("blk")
     part = (tiles_dev, tile_rows, row_width)
     dest_tiles = groups * tiles_dev
-    source = scale_rows(embed_codes.reshape(part), embed_exps, degrees)
+    source, factors = scale_rows(embed_codes.reshape(part), embed_exps, degrees)
 
     def across(value, hop):
         pairs = [
@@ -234,27 +262,35 @@
     )(order, early, blocks)
     *middle, total = lax.optimization_barrier((*middle, total))
     panels = middle + [other] + [paired(panel, "blk", 1) for panel in middle]
-    far = pl.pallas_call(
-        far_kernel,
-        out_shape=jax.ShapeDtypeStruct((far_tiles, tile_rows, row_width), jnp.bfloat16),
+    half = tiles_dev // 2
+    low, high = (half, tile_rows, row_width), (tiles_dev - half, tile_rows, row_width)
+    far, far_high = pl.pallas_call(
+        functools.partial(far_kernel, half),
+        out_shape=[
+            jax.ShapeDtypeStruct((len(far_chunks),) + low, jnp.bfloat16),
+            jax.ShapeDtypeStruct((len(far_chunks),) + high, jnp.bfloat16),
+        ],
         in_specs=[SMEM] + [VMEM] * (len(panels) + 2),
-        out_specs=VMEM,
+        out_specs=[VMEM] * 2,
         scratch_shapes=[held(len(panels) * tiles_dev, jnp.bfloat16)],
         compiler_params=LIMIT,
         cost_estimate=cost_of(capacity // 8, tile_rows, row_width),
     )(order, *panels, blocks, total)
-    far, order = lax.optimization_barrier((far, order))
-    far_arrived = paired(far, "grp", 1).reshape((len(far_chunks),) + part)
+    far, far_high, order = lax.optimization_barrier((far, far_high, order))
+    far_arrived = paired(far, "grp", 1)
+    highs = [paired(far_high[at], "grp", hop) for at, hop in enumerate(far_chunks)]
     panels = [early] + panels
-    own, near, mine = pl.pallas_call(
-        functools.partial(rest_kernel, tiles_dev, mine_chunks),
+    own_low, own_high, near, mine, mine_high = pl.pallas_call(
+        functools.partial(rest_kernel, half, mine_chunks),
         out_shape=[
-            jax.ShapeDtypeStruct(part, jnp.float32),
+            jax.ShapeDtypeStruct(low, jnp.float32),
+            jax.ShapeDtypeStruct(high, jnp.float32),
             jax.ShapeDtypeStruct(part, jnp.bfloat16),
-            jax.ShapeDtypeStruct((len(mine_chunks),) + part, jnp.float32),
+            jax.ShapeDtypeStruct((len(mine_chunks),) + low, jnp.float32),
+            jax.ShapeDtypeStruct((len(mine_chunks),) + high, jnp.bfloat16),
         ],
         in_specs=[SMEM] + [VMEM] * (len(panels) + 1),
-        out_specs=[VMEM] * 3,
+        out_specs=[VMEM] * 5,
         scratch_shapes=[
             held(len(panels) * tiles_dev, jnp.bfloat16),
             held(dest_tiles + 1, jnp.float32),
@@ -262,14 +298,30 @@
         compiler_params=LIMIT,
         cost_estimate=cost_of(capacity, tile_rows, row_width),
     )(order, *panels, blocks)
-    summed = own
+    mine_arrived = [paired(mine_high[at], "grp", hop) for at, hop in enumerate(mine_chunks)]
+    lows = []
     for at, hop in enumerate(mine_chunks):
         pair = (mine[at] + far_arrived[at].astype(jnp.float32)).astype(jnp.bfloat16)
         near, pair = lax.optimization_barrier((near, pair))
-        summed = summed + paired(pair, "grp", hop).astype(jnp.float32)
-    summed = summed + paired(near, "grp", 1).astype(jnp.float32)
-    inverse = lax.rsqrt(degrees.astype(jnp.float32))
-    return (summed.reshape(1, row_count, row_width) * inverse[..., None]).astype(jnp.bfloat16)
+        lows.append(paired(pair, "grp", hop))
+    near_arrived = paired(near, "grp", 1)
+    own_high = own_high + sum(piece.astype(jnp.float32) for piece in highs)
+    own_high, near_arrived, *tails = lax.optimization_barrier(
+        (own_high, near_arrived, *lows, *mine_arrived)
+    )
+    out = pl.pallas_call(
+        final_kernel,
+        out_shape=jax.ShapeDtypeStruct(part, jnp.bfloat16),
+        in_specs=[VMEM] * (4 + len(tails)),
+        out_specs=HBM,
+        scratch_shapes=[
+            held(tiles_dev, jnp.bfloat16),
+            pltpu.SemaphoreType.DMA((tiles_dev,)),
+        ],
+        compiler_params=LIMIT,
+        cost_estimate=cost_of(0, tile_rows, row_width),
+    )(factors, near_arrived, own_low, own_high, *tails)
+    return out.reshape(1, row_count, row_width)
 
 
 def solution(mesh):

time: 30.2 us -> 31.7 us (1.050); the launches traced: 29.8 us -> 31.9 us
  starting transfers between devices: 10.6 us -> 12.8 us
  Pallas kernels: 8.15 us -> 9.11 us
  other arithmetic: 0.94 us -> 0.11 us
    ppermute x5 -> x7, starting transfers between devices: 6.14 us -> 8.33 us  [paired(): lax.ppermute(value, axis, [(at, at ^ hop) for at in range(lax.axis_size(a...]
    convert_element_type x1 -> x0, other arithmetic: 0.79 us -> none  [shards(): (summed.reshape(1, row_count, row_width) * inverse[..., None]).astype(jnp...]
    pallas_call x1, Pallas kernels: 0.59 us -> 1.07 us  [shards(): pl.pallas_call(early_kernel, out_shape=jax.ShapeDtypeStruct((far_tiles +...]
    pallas_call x3 -> x4, Pallas kernels: 3.95 us -> 4.43 us  [the longest x1 2.14 us: shards(): pl.pallas_call(functools.partial(rest_kernel, half, mine_chunks), out_sha...]
    ppermute x2, waiting for transfers between devices: 1.72 us -> 1.24 us  [across(): return lax.ppermute(value, ('side', 'blk'), pairs)]
    ppermute x5 -> x7, waiting for transfers between devices: 8.27 us -> 8.52 us  [paired(): lax.ppermute(value, axis, [(at, at ^ hop) for at in range(lax.axis_size(a...]
  transfers between devices with their start and end apart: 7 -> 9, of which waited for: 7 -> 6; matrix products, arithmetic and copies ran while one was open for 0% -> 0% of each run, Pallas kernels for 20% -> 21%
where the time goes in v2:
time: 31.7 us; the launch traced here: 31.9 us
  starting transfers between devices  12.8 us (40%)
  waiting for transfers between devices  9.76 us (31%)
  Pallas kernels  9.11 us (29%)
    ppermute x7, waiting for transfers between devices, paired(): lax.ppermute(value, axis, [(at, at ^ hop) for at in range(lax.axis_size(a...  8.52 us
    ppermute x7, starting transfers between devices, paired(): lax.ppermute(value, axis, [(at, at ^ hop) for at in range(lax.axis_size(a...  8.33 us
    ppermute x2, starting transfers between devices, across(): return lax.ppermute(value, ('side', 'blk'), pairs)  4.49 us
    pallas_call x1, Pallas kernels, stage_blocks(): pl.pallas_call(functools.partial(stage_kernel, blks, groups, tiles_dev),...  3.61 us
    pallas_call x1, Pallas kernels, shards(): pl.pallas_call(functools.partial(rest_kernel, half, mine_chunks), out_sha...  2.14 us
    ppermute x2, waiting for transfers between devices, across(): return lax.ppermute(value, ('side', 'blk'), pairs)  1.24 us
    pallas_call x1, Pallas kernels, shards(): pl.pallas_call(early_kernel, out_shape=jax.ShapeDtypeStruct((far_tiles +...  1.07 us
    pallas_call x1, Pallas kernels, scale_rows(): pl.pallas_call(scale_kernel, out_shape=[jax.ShapeDtypeStruct(codes.shape,...  0.98 us
  transfers between devices with their start and end apart: 9, of which 6 were waited for; matrix products, arithmetic and copies ran while one was open for 0% of the time, Pallas kernels for 21%

profile of v2, /device:TPU:0, one launch (start us, length us, event | category | flops | bytes accessed | tf_op | source)
XLA Modules:
  0.0 31.9 jit_solution(12475663406789447176)
XLA Ops:
  0.0 1.0 %shard_map.55 = (bf16[4,128,128]{2,1,0:T(8,128)(2,1)S(1)}, f32[4,128,128]{2,1,0:T(8,128)S(1)}) custom-call(s32[1,4]{1,0:T(1,128)} %exps_hbm.1, s32[1,512]{1,0:T(1,128)} %degrees_hbm.1, bf16[4,128,128]{2,1,0:T(8,128)(2,1)} %bitcast.13), custom_call_target="tpu_custom_call" | custom-call | flops 65536 | bytes 262144 | tf_op jit(solution)/shard_map/pallas_call | solution.py:51
  1.0 4.0 %collective-permute-start = (bf16[4,128,128]{2,1,0:T(8,128)(2,1)S(1)}, bf16[4,128,128]{2,1,0:T(8,128)(2,1)S(1)}, u32[]{:S(2)}, u32[]{:S(2)}) collective-permute-start(bf16[4,128,128]{2,1,0:T(8,128)(2,1)S(1)} %get-tuple-element.30), channel_id=1, source_target_pairs={{0,18},{1,19},{2,16},{3,17},{16,2},{17,3},{18,0},{19,1},{4,22},{5,... | collective-permute-start | bytes 393224 | tf_op jit(solution)/shard_map/ppermute | solution.py:239
  5.0 0.5 %collective-permute-start.1 = (bf16[4,128,128]{2,1,0:T(8,128)(2,1)S(1)}, bf16[4,128,128]{2,1,0:T(8,128)(2,1)S(1)}, u32[]{:S(2)}, u32[]{:S(2)}) collective-permute-start(bf16[4,128,128]{2,1,0:T(8,128)(2,1)S(1)} %get-tuple-element.30), channel_id=1, source_target_pairs={{0,16},{1,17},{2,18},{3,19},{16,0},{17,1},{18,2},{19,3},{4,20},{5,... | collective-permute-start | bytes 393224 | tf_op jit(solution)/shard_map/ppermute | solution.py:239
  5.5 0.1 pad_add_fusion.place_ref
  5.6 3.6 %shard_map.56 = (s32[4,112]{1,0:T(4,128)S(1)}, bf16[96,128,128]{2,1,0:T(8,128)(2,1)S(1)}) custom-call(s32[2]{0:T(128)S(1)} %pad_add_fusion.place_ref, s32[2,96]{1,0:T(2,128)} %bitcast.14, bf16[96,128,128]{2,1,0:T(8,128)(2,1)} %bitcast.12), custom_call_target="tpu_custom_call" | custom-call | tf_op jit(solution)/shard_map/pallas_call | solution.py:130
  9.2 0.1 collective-permute-done.panel.refs_0_
  9.3 0.0 collective-permute-start.2
  9.3 1.1 %shard_map.57.refs_4_ = f32[5,128,128]{2,1,0:T(8,128)S(1)} custom-call(s32[4,112]{1,0:T(4,128)S(1)} %get-tuple-element.39.order_ref, bf16[4,128,128]{2,1,0:T(8,128)(2,1)S(1)} %collective-permute-done.panel.refs_0_, bf16[96,128,128]{2,1,0:T(8,128)(2,1)S(1)} %get-tuple-element.34.blocks.refs_3_.refs_4_), custom_call_target="tpu_custom_call" | custom-call | flops 50331648 | bytes 393216 | tf_op jit(solution)/shard_map/pallas_call | solution.py:255
  10.4 1.1 %collective-permute-done.1.refs_0_.refs_1_ = bf16[4,128,128]{2,1,0:T(8,128)(2,1)S(1)} collective-permute-done((bf16[4,128,128]{2,1,0:T(8,128)(2,1)S(1)}, bf16[4,128,128]{2,1,0:T(8,128)(2,1)S(1)}, u32[]{:S(2)}, u32[]{:S(2)}) %collective-permute-start.1) | collective-permute-done | bytes 131104 | tf_op jit(solution)/shard_map/ppermute | solution.py:239
  11.5 0.0 collective-permute-start.3
  11.5 0.0 collective-permute-done.2.refs_1_.refs_2_
  11.5 1.3 %collective-permute-done.3.refs_2_.refs_3_ = bf16[4,128,128]{2,1,0:T(8,128)(2,1)S(1)} collective-permute-done((bf16[4,128,128]{2,1,0:T(8,128)(2,1)S(1)}, bf16[4,128,128]{2,1,0:T(8,128)(2,1)S(1)}, u32[]{:S(2)}, u32[]{:S(2)}) %collective-permute-start.3) | collective-permute-done | bytes 131104 | tf_op jit(solution)/shard_map/ppermute | solution.py:242
  12.9 0.6 %shard_map.58 = (bf16[1,2,128,128]{3,2,1,0:T(8,128)(2,1)S(1)}, bf16[1,2,128,128]{3,2,1,0:T(8,128)(2,1)S(1)}) custom-call(s32[4,112]{1,0:T(4,128)S(1)} %get-tuple-element.39.order_ref, bf16[4,128,128]{2,1,0:T(8,128)(2,1)S(1)} %collective-permute-done.1.refs_0_.refs_1_, bf16[4,128,128]{2,1,0:T(8,128)(2,1)S(1)} %collective-permute-done.2.refs_1_.refs_2_, ...), custom_call_target="tpu_custom_call" | custom-call | flops 50331648 | bytes 393216 | tf_op jit(solution)/shard_map/pallas_call | solution.py:267
  13.5 1.9 %collective-permute-start.5 = (bf16[1,2,128,128]{3,2,1,0:T(8,128)(2,1)S(1)}, bf16[1,2,128,128]{3,2,1,0:T(8,128)(2,1)S(1)}, u32[]{:S(2)}, u32[]{:S(2)}) collective-permute-start(bf16[1,2,128,128]{3,2,1,0:T(8,128)(2,1)S(1)} %get-tuple-element.44), channel_id=1, source_target_pairs={{0,4},{4,0},{8,12},{12,8},{1,5},{5,1},{9,13},{13,9},{2,6},{6,2},{1... | collective-permute-start | bytes 196616 | tf_op jit(solution)/shard_map/ppermute | solution.py:242
  15.4 2.7 %collective-permute-start.4 = (bf16[2,128,128]{2,1,0:T(8,128)(2,1)S(1)}, bf16[2,128,128]{2,1,0:T(8,128)(2,1)S(1)}, u32[]{:S(2)}, u32[]{:S(2)}) collective-permute-start(bf16[2,128,128]{2,1,0:T(8,128)(2,1)S(1)} %bitcast.10), channel_id=1, source_target_pairs={{0,12},{4,8},{8,4},{12,0},{1,13},{5,9},{9,5},{13,1},{2,14},{6,10},... | collective-permute-start | bytes 196616 | tf_op jit(solution)/shard_map/ppermute | solution.py:242
  18.1 2.1 %shard_map.59 = (f32[2,128,128]{2,1,0:T(8,128)S(1)}, f32[2,128,128]{2,1,0:T(8,128)S(1)}, bf16[4,128,128]{2,1,0:T(8,128)(2,1)S(1)}, f32[1,2,128,128]{3,2,1,0:T(8,128)S(1)}, bf16[1,2,128,128]{3,2,1,0:T(8,128)(2,1)S(1)}) custom-call(s32[4,112]{1,0:T(4,128)S(1)} %get-tuple-element.39.order_ref, bf16[4,128,128]{2,1,0:T(8,128)(2,1)S(1)} %collective-permute-done.panel.refs_0_, ...), custom_call_target="tpu_custom_call" | custom-call | flops 402653184 | bytes 3145728 | tf_op jit(solution)/shard_map/pallas_call | solution.py:283
  20.2 0.4 %collective-permute-start.8 = (bf16[2,128,128]{2,1,0:T(8,128)(2,1)S(1)}, bf16[2,128,128]{2,1,0:T(8,128)(2,1)S(1)}, u32[]{:S(2)}, u32[]{:S(2)}) collective-permute-start(bf16[2,128,128]{2,1,0:T(8,128)(2,1)S(1)} %bitcast.11), channel_id=1, source_target_pairs={{0,8},{4,12},{8,0},{12,4},{1,9},{5,13},{9,1},{13,5},{2,10},{6,14},... | collective-permute-start | bytes 196616 | tf_op jit(solution)/shard_map/ppermute | solution.py:242
  20.6 0.0 collective-permute-done.5
  20.7 2.6 %collective-permute-start.7 = (bf16[2,128,128]{2,1,0:T(8,128)(2,1)S(1)}, bf16[2,128,128]{2,1,0:T(8,128)(2,1)S(1)}, u32[]{:S(2)}, u32[]{:S(2)}) collective-permute-start(bf16[2,128,128]{2,1,0:T(8,128)(2,1)S(1)} %fusion), channel_id=1, source_target_pairs={{0,8},{4,12},{8,0},{12,4},{1,9},{5,13},{9,1},{13,5},{2,10},{6,14},... | collective-permute-start | bytes 196616 | tf_op jit(solution)/shard_map/ppermute | solution.py:242
  23.3 0.7 %collective-permute-start.6 = (bf16[4,128,128]{2,1,0:T(8,128)(2,1)S(1)}, bf16[4,128,128]{2,1,0:T(8,128)(2,1)S(1)}, u32[]{:S(2)}, u32[]{:S(2)}) collective-permute-start(bf16[4,128,128]{2,1,0:T(8,128)(2,1)S(1)} %get-tuple-element.45), channel_id=1, source_target_pairs={{0,4},{4,0},{8,12},{12,8},{1,5},{5,1},{9,13},{13,9},{2,6},{6,2},{1... | collective-permute-start | bytes 393224 | tf_op jit(solution)/shard_map/ppermute | solution.py:242
  24.0 4.3 %collective-permute-done.8.refs_1_ = bf16[2,128,128]{2,1,0:T(8,128)(2,1)S(1)} collective-permute-done((bf16[2,128,128]{2,1,0:T(8,128)(2,1)S(1)}, bf16[2,128,128]{2,1,0:T(8,128)(2,1)S(1)}, u32[]{:S(2)}, u32[]{:S(2)}) %collective-permute-start.8) | collective-permute-done | bytes 65568 | tf_op jit(solution)/shard_map/ppermute | solution.py:242
  28.3 1.3 %collective-permute-done.7.refs_0_ = bf16[2,128,128]{2,1,0:T(8,128)(2,1)S(1)} collective-permute-done((bf16[2,128,128]{2,1,0:T(8,128)(2,1)S(1)}, bf16[2,128,128]{2,1,0:T(8,128)(2,1)S(1)}, u32[]{:S(2)}, u32[]{:S(2)}) %collective-permute-start.7) | collective-permute-done | bytes 65568 | tf_op jit(solution)/shard_map/ppermute | solution.py:242
  29.6 1.6 %collective-permute-done.6.near = bf16[4,128,128]{2,1,0:T(8,128)(2,1)S(1)} collective-permute-done((bf16[4,128,128]{2,1,0:T(8,128)(2,1)S(1)}, bf16[4,128,128]{2,1,0:T(8,128)(2,1)S(1)}, u32[]{:S(2)}, u32[]{:S(2)}) %collective-permute-start.6) | collective-permute-done | bytes 131104 | tf_op jit(solution)/shard_map/ppermute | solution.py:242
  31.2 0.7 %shard_map.60 = bf16[4,128,128]{2,1,0:T(8,128)(2,1)} custom-call(f32[4,128,128]{2,1,0:T(8,128)S(1)} %get-tuple-element.29.factors, bf16[4,128,128]{2,1,0:T(8,128)(2,1)S(1)} %collective-permute-done.6.near, f32[2,128,128]{2,1,0:T(8,128)S(1)} %get-tuple-element.49.own_low, f32[2,128,128]{2,1,0:T(8,128)S(1)} %convert_add_fusion.own_high, ...), custom_call_target="tpu_custom_call" | custom-call | tf_op jit(solution)/shard_map/pallas_call | solution.py:312
  (3 shorter events, 0.0 us)
Async XLA Ops:
  1.0 8.3 %collective-permute-start = (bf16[4,128,128]{2,1,0:T(8,128)(2,1)S(1)}, bf16[4,128,128]{2,1,0:T(8,128)(2,1)S(1)}, u32[]{:S(2)}, u32[]{:S(2)}) collective-permute-start(bf16[4,128,128]{2,1,0:T(8,128)(2,1)S(1)} %get-tuple-element.30), channel_id=1, source_target_pairs={{0,18},{1,19},{2,16},{3,17},{16,2},{17,3},{18,0},{19,1},{4,22},{5,... | collective-permute-start | bytes 393224 | tf_op jit(solution)/shard_map/ppermute | solution.py:239
  5.0 6.6 %collective-permute-start.1 = (bf16[4,128,128]{2,1,0:T(8,128)(2,1)S(1)}, bf16[4,128,128]{2,1,0:T(8,128)(2,1)S(1)}, u32[]{:S(2)}, u32[]{:S(2)}) collective-permute-start(bf16[4,128,128]{2,1,0:T(8,128)(2,1)S(1)} %get-tuple-element.30), channel_id=1, source_target_pairs={{0,16},{1,17},{2,18},{3,19},{16,0},{17,1},{18,2},{19,3},{4,20},{5,... | collective-permute-start | bytes 393224 | tf_op jit(solution)/shard_map/ppermute | solution.py:239
  9.3 2.2 %collective-permute-start.2 = (bf16[4,128,128]{2,1,0:T(8,128)(2,1)S(1)}, bf16[4,128,128]{2,1,0:T(8,128)(2,1)S(1)}, u32[]{:S(2)}, u32[]{:S(2)}) collective-permute-start(bf16[4,128,128]{2,1,0:T(8,128)(2,1)S(1)} %collective-permute-done.panel.refs_0_), channel_id=1, source_target_pairs={{0,1},{1,0},{2,3},{3,2},{4,5},{5,4},{6,7},{7,6},{8,9},{9,8},{10,11... | collective-permute-start | bytes 393224 | tf_op jit(solution)/shard_map/ppermute | solution.py:242
  11.5 1.3 %collective-permute-start.3 = (bf16[4,128,128]{2,1,0:T(8,128)(2,1)S(1)}, bf16[4,128,128]{2,1,0:T(8,128)(2,1)S(1)}, u32[]{:S(2)}, u32[]{:S(2)}) collective-permute-start(bf16[4,128,128]{2,1,0:T(8,128)(2,1)S(1)} %collective-permute-done.1.refs_0_.refs_1_), channel_id=1, source_target_pairs={{0,1},{1,0},{2,3},{3,2},{4,5},{5,4},{6,7},{7,6},{8,9},{9,8},{10,11... | collective-permute-start | bytes 393224 | tf_op jit(solution)/shard_map/ppermute | solution.py:242
  13.5 7.2 %collective-permute-start.5 = (bf16[1,2,128,128]{3,2,1,0:T(8,128)(2,1)S(1)}, bf16[1,2,128,128]{3,2,1,0:T(8,128)(2,1)S(1)}, u32[]{:S(2)}, u32[]{:S(2)}) collective-permute-start(bf16[1,2,128,128]{3,2,1,0:T(8,128)(2,1)S(1)} %get-tuple-element.44), channel_id=1, source_target_pairs={{0,4},{4,0},{8,12},{12,8},{1,5},{5,1},{9,13},{13,9},{2,6},{6,2},{1... | collective-permute-start | bytes 196616 | tf_op jit(solution)/shard_map/ppermute | solution.py:242
  15.4 8.6 %collective-permute-start.4 = (bf16[2,128,128]{2,1,0:T(8,128)(2,1)S(1)}, bf16[2,128,128]{2,1,0:T(8,128)(2,1)S(1)}, u32[]{:S(2)}, u32[]{:S(2)}) collective-permute-start(bf16[2,128,128]{2,1,0:T(8,128)(2,1)S(1)} %bitcast.10), channel_id=1, source_target_pairs={{0,12},{4,8},{8,4},{12,0},{1,13},{5,9},{9,5},{13,1},{2,14},{6,10},... | collective-permute-start | bytes 196616 | tf_op jit(solution)/shard_map/ppermute | solution.py:242
  20.2 8.1 %collective-permute-start.8 = (bf16[2,128,128]{2,1,0:T(8,128)(2,1)S(1)}, bf16[2,128,128]{2,1,0:T(8,128)(2,1)S(1)}, u32[]{:S(2)}, u32[]{:S(2)}) collective-permute-start(bf16[2,128,128]{2,1,0:T(8,128)(2,1)S(1)} %bitcast.11), channel_id=1, source_target_pairs={{0,8},{4,12},{8,0},{12,4},{1,9},{5,13},{9,1},{13,5},{2,10},{6,14},... | collective-permute-start | bytes 196616 | tf_op jit(solution)/shard_map/ppermute | solution.py:242
  20.7 9.0 %collective-permute-start.7 = (bf16[2,128,128]{2,1,0:T(8,128)(2,1)S(1)}, bf16[2,128,128]{2,1,0:T(8,128)(2,1)S(1)}, u32[]{:S(2)}, u32[]{:S(2)}) collective-permute-start(bf16[2,128,128]{2,1,0:T(8,128)(2,1)S(1)} %fusion), channel_id=1, source_target_pairs={{0,8},{4,12},{8,0},{12,4},{1,9},{5,13},{9,1},{13,5},{2,10},{6,14},... | collective-permute-start | bytes 196616 | tf_op jit(solution)/shard_map/ppermute | solution.py:242
  23.3 7.9 %collective-permute-start.6 = (bf16[4,128,128]{2,1,0:T(8,128)(2,1)S(1)}, bf16[4,128,128]{2,1,0:T(8,128)(2,1)S(1)}, u32[]{:S(2)}, u32[]{:S(2)}) collective-permute-start(bf16[4,128,128]{2,1,0:T(8,128)(2,1)S(1)} %get-tuple-element.45), channel_id=1, source_target_pairs={{0,4},{4,0},{8,12},{12,8},{1,5},{5,1},{9,13},{13,9},{2,6},{6,2},{1... | collective-permute-start | bytes 393224 | tf_op jit(solution)/shard_map/ppermute | solution.py:242

commit v3 on v1

--- a/solution.py
+++ b/solution.py
@@ -8,7 +8,7 @@
 from jax.sharding import PartitionSpec as P
 
 UNROLL = 8
-STAGES = 3
+STAGES = 4
 VMEM = pl.BlockSpec(memory_space=pltpu.VMEM)
 SMEM = pl.BlockSpec(memory_space=pltpu.SMEM)
 HBM = pl.BlockSpec(memory_space=pltpu.HBM)
@@ -25,7 +25,7 @@
     return value // size, value % size
 
 
-def scale_kernel(exps_hbm, degrees_hbm, codes_hbm, rows, exps_ref, degrees, codes, sems):
+def scale_kernel(exps_hbm, degrees_hbm, codes_hbm, rows, factors, exps_ref, degrees, codes, sems):
     pairs = [(exps_hbm, exps_ref), (degrees_hbm, degrees), (codes_hbm, codes)]
     fetches = [
         pltpu.make_async_copy(held, wanted, sems.at[at])
@@ -37,22 +37,25 @@
     fetches[1].wait()
     tiles_dev, tile_rows, row_width = rows.shape
     inverse = lax.rsqrt(degrees[...].astype(jnp.float32))
-    factors = []
     for tile in range(tiles_dev):
         lanes = inverse[:, tile * tile_rows : (tile + 1) * tile_rows]
-        scale = jnp.exp2(jnp.full(lanes.shape, exps_ref[0, tile], jnp.int32).astype(jnp.float32))
-        factors.append(jnp.broadcast_to(lanes * scale, (row_width, tile_rows)).T)
+        factors[tile] = jnp.broadcast_to(lanes, (row_width, tile_rows)).T
     fetches[2].wait()
-    for tile, factor in enumerate(factors):
-        rows[tile] = (codes[tile].astype(jnp.float32) * factor).astype(rows.dtype)
+    for tile in range(tiles_dev):
+        scale = jnp.exp2(jnp.full((1, 1), exps_ref[0, tile], jnp.int32).astype(jnp.float32))
+        scaled = codes[tile].astype(jnp.float32) * scale * factors[tile]
+        rows[tile] = scaled.astype(rows.dtype)
 
 
 def scale_rows(codes, exps, degrees):
     return pl.pallas_call(
         scale_kernel,
-        out_shape=jax.ShapeDtypeStruct(codes.shape, jnp.bfloat16),
+        out_shape=[
+            jax.ShapeDtypeStruct(codes.shape, jnp.bfloat16),
+            jax.ShapeDtypeStruct(codes.shape, jnp.float32),
+        ],
         in_specs=[HBM] * 3,
-        out_specs=VMEM,
+        out_specs=[VMEM] * 2,
         scratch_shapes=[
             pltpu.SMEM(exps.shape, exps.dtype),
             pltpu.VMEM(degrees.shape, degrees.dtype),
@@ -90,10 +93,10 @@
         rank = half - 1 - (hop >> 1)
         odd = hop & 1
         far = (chunk >= 2) & ((chunk & 1) == 1)
-        stage = jnp.where(far, jnp.minimum(rank + odd, 1), 2)
+        stage = jnp.where(far, jnp.minimum(rank + odd, 1), jnp.where(chunk >= 2, 2, 3))
         stage = jnp.where(origin < source_tiles, stage, STAGES)
         panel = rank + odd * half - (stage == 1).astype(jnp.int32)
-        kept = jnp.where(far, (chunk - 3) >> 1, chunk)
+        kept = jnp.where(chunk >= 2, (chunk >> 1) - 1, chunk)
         word = pack(slot, panel * tiles_dev + row, kept * tiles_dev + tile)
         where = jnp.int32(0)
         for at, position in enumerate(nexts):
@@ -105,7 +108,7 @@
 
     ends = lax.fori_loop(0, capacity, enlist, (jnp.int32(0),) * STAGES, unroll=8)
     far_tiles = (groups // 2 - 1) * tiles_dev
-    spares = [pack(0, 0, far_tiles)] * 2 + [pack(0, 0, groups * tiles_dev)]
+    spares = [pack(0, 0, far_tiles)] * 3 + [pack(0, 0, 2 * tiles_dev)]
     for at, (end, spare) in enumerate(zip(ends, spares)):
         for extra in range(UNROLL):
             order_ref[at, end + extra] = spare
@@ -171,15 +174,35 @@
     far[...] = total[: far.shape[0]].astype(far.dtype)
 
 
-def rest_kernel(tiles_dev, chunks, order_ref, *refs):
-    *panels, blocks, own, near, mine, source, total = refs
+def mine_kernel(order_ref, *refs):
+    *panels, blocks, total, mine, source = refs
     gather_panels(panels, source)
     total[...] = jnp.zeros_like(total)
     add_products(2, order_ref, blocks, source, total)
-    own[...] = total[:tiles_dev]
-    near[...] = total[tiles_dev : 2 * tiles_dev].astype(near.dtype)
-    for at, chunk in enumerate(chunks):
-        mine[at] = total[chunk * tiles_dev : (chunk + 1) * tiles_dev]
+    mine[...] = total[: mine.shape[0]].astype(mine.dtype)
+
+
+def near_kernel(order_ref, *refs):
+    *panels, blocks, own, near, source, total = refs
+    gather_panels(panels, source)
+    total[...] = jnp.zeros_like(total)
+    add_products(3, order_ref, blocks, source, total)
+    own[...] = total[: own.shape[0]]
+    near[...] = total[own.shape[0] : 2 * own.shape[0]].astype(near.dtype)
+
+
+def final_kernel(factors, own, *refs):
+    *arrived, out_hbm, out, sems = refs
+    copies = []
+    for tile in range(out.shape[0]):
+        value = own[tile]
+        for piece in arrived:
+            value = value + piece[tile].astype(jnp.float32)
+        out[tile] = (value * factors[tile]).astype(out.dtype)
+        copies.append(pltpu.make_async_copy(out.at[tile], out_hbm.at[tile], sems.at[tile]))
+        copies[-1].start()
+    for copy in copies:
+        copy.wait()
 
 
 def cost_of(slots, tile_rows, row_width):
@@ -199,8 +222,7 @@
     groups = lax.axis_size("grp")
     blks = lax.axis_size("blk")
     part = (tiles_dev, tile_rows, row_width)
-    dest_tiles = groups * tiles_dev
-    source = scale_rows(embed_codes.reshape(part), embed_exps, degrees)
+    source, factors = scale_rows(embed_codes.reshape(part), embed_exps, degrees)
 
     def across(value, hop):
         pairs = [
@@ -244,32 +266,68 @@
         cost_estimate=cost_of(capacity // 8, tile_rows, row_width),
     )(order, *panels, blocks, total)
     far, order = lax.optimization_barrier((far, order))
-    far_arrived = paired(far, "grp", 1).reshape((len(far_chunks),) + part)
     panels = [early] + panels
-    own, near, mine = pl.pallas_call(
-        functools.partial(rest_kernel, tiles_dev, mine_chunks),
+    mine_total, mine = pl.pallas_call(
+        mine_kernel,
+        out_shape=[
+            jax.ShapeDtypeStruct((far_tiles + 1, tile_rows, row_width), jnp.float32),
+            jax.ShapeDtypeStruct((far_tiles, tile_rows, row_width), jnp.bfloat16),
+        ],
+        in_specs=[SMEM] + [VMEM] * (len(panels) + 1),
+        out_specs=[VMEM] * 2,
+        scratch_shapes=[held(len(panels) * tiles_dev, jnp.bfloat16)],
+        compiler_params=LIMIT,
+        cost_estimate=cost_of(capacity // 4, tile_rows, row_width),
+    )(order, *panels, blocks)
+    mine, order = lax.optimization_barrier((mine, order))
+    own, near = pl.pallas_call(
+        near_kernel,
         out_shape=[
             jax.ShapeDtypeStruct(part, jnp.float32),
             jax.ShapeDtypeStruct(part, jnp.bfloat16),
-            jax.ShapeDtypeStruct((len(mine_chunks),) + part, jnp.float32),
         ],
         in_specs=[SMEM] + [VMEM] * (len(panels) + 1),
-        out_specs=[VMEM] * 3,
+        out_specs=[VMEM] * 2,
         scratch_shapes=[
             held(len(panels) * tiles_dev, jnp.bfloat16),
-            held(dest_tiles + 1, jnp.float32),
-        ],
-        compiler_params=LIMIT,
-        cost_estimate=cost_of(capacity, tile_rows, row_width),
+            held(2 * tiles_dev + 1, jnp.float32),
+        ],
+        compiler_params=LIMIT,
+        cost_estimate=cost_of(capacity // 2, tile_rows, row_width),
     )(order, *panels, blocks)
-    summed = own
+
+    def outer(at, owner):
+        return abs(at - owner) > abs((at ^ 1) - owner)
+
+    def sent(value, way, hop, wanted):
+        pairs = [(at, at ^ way) for at in range(groups) if outer(at, at ^ hop) == wanted]
+        return lax.ppermute(value, "grp", pairs)
+
+    straight, sums = [], []
     for at, hop in enumerate(mine_chunks):
-        pair = (mine[at] + far_arrived[at].astype(jnp.float32)).astype(jnp.bfloat16)
+        piece = slice(at * tiles_dev, (at + 1) * tiles_dev)
+        handed = sent(far[piece], 1, hop + 1, True)
+        straight.append(sent(far[piece], hop + 1, hop + 1, False))
+        straight.append(sent(mine[piece], hop, hop, True))
+        pair = (mine_total[piece] + handed.astype(jnp.float32)).astype(jnp.bfloat16)
         near, pair = lax.optimization_barrier((near, pair))
-        summed = summed + paired(pair, "grp", hop).astype(jnp.float32)
-    summed = summed + paired(near, "grp", 1).astype(jnp.float32)
-    inverse = lax.rsqrt(degrees.astype(jnp.float32))
-    return (summed.reshape(1, row_count, row_width) * inverse[..., None]).astype(jnp.bfloat16)
+        sums.append(sent(pair, hop, hop, False))
+    near_arrived = paired(near, "grp", 1)
+    own = own + sum(piece.astype(jnp.float32) for piece in straight)
+    own, near_arrived, *sums = lax.optimization_barrier((own, near_arrived, *sums))
+    out = pl.pallas_call(
+        final_kernel,
+        out_shape=jax.ShapeDtypeStruct(part, jnp.bfloat16),
+        in_specs=[VMEM] * (3 + len(sums)),
+        out_specs=HBM,
+        scratch_shapes=[
+            held(tiles_dev, jnp.bfloat16),
+            pltpu.SemaphoreType.DMA((tiles_dev,)),
+        ],
+        compiler_params=LIMIT,
+        cost_estimate=cost_of(0, tile_rows, row_width),
+    )(factors, own, near_arrived, *sums)
+    return out.reshape(1, row_count, row_width)
 
 
 def solution(mesh):

time: 30.2 us -> 34.2 us (1.13); the launches traced: 29.8 us -> 34.1 us
  starting transfers between devices: 10.6 us -> 14.1 us
  Pallas kernels: 8.15 us -> 10.6 us
  waiting for transfers between devices: 9.99 us -> 9.19 us
  other arithmetic: 0.94 us -> 0.15 us
    ppermute x0 -> x4, starting transfers between devices: none -> 9.43 us  [sent(): return lax.ppermute(value, 'grp', pairs)]
    ppermute x5 -> x3, starting transfers between devices: 6.14 us -> 0.14 us  [paired(): lax.ppermute(value, axis, [(at, at ^ hop) for at in range(lax.axis_size(a...]
    ppermute x5 -> x3, waiting for transfers between devices: 8.27 us -> 5.04 us  [paired(): lax.ppermute(value, axis, [(at, at ^ hop) for at in range(lax.axis_size(a...]
    ppermute x0 -> x4, waiting for transfers between devices: none -> 2.82 us  [sent(): return lax.ppermute(value, 'grp', pairs)]
    pallas_call x2 -> x4, Pallas kernels: 2.86 us -> 4.96 us  [the longest x1 1.89 us: shards(): pl.pallas_call(near_kernel, out_shape=[jax.ShapeDtypeStruct(part, jnp.flo...]
    convert_element_type x2 -> x1, other arithmetic: 0.82 us -> 0.03 us  [shards(): pair = (mine_total[piece] + handed.astype(jnp.float32)).astype(jnp.bfloat16)]
    ppermute x2, waiting for transfers between devices: 1.72 us -> 1.34 us  [across(): return lax.ppermute(value, ('side', 'blk'), pairs)]
  transfers between devices with their start and end apart: 7 -> 9, of which waited for: 7 -> 4; matrix products, arithmetic and copies ran while one was open for 0% -> 0% of each run, Pallas kernels for 20% -> 23%
where the time goes in v3:
time: 34.2 us; the launch traced here: 34.1 us
  starting transfers between devices  14.1 us (41%)
  Pallas kernels  10.6 us (31%)
  waiting for transfers between devices  9.19 us (27%)
    ppermute x4, starting transfers between devices, sent(): return lax.ppermute(value, 'grp', pairs)  9.43 us
    ppermute x3, waiting for transfers between devices, paired(): lax.ppermute(value, axis, [(at, at ^ hop) for at in range(lax.axis_size(a...  5.04 us
    ppermute x2, starting transfers between devices, across(): return lax.ppermute(value, ('side', 'blk'), pairs)  4.49 us
    pallas_call x1, Pallas kernels, stage_blocks(): pl.pallas_call(functools.partial(stage_kernel, blks, groups, tiles_dev),...  3.88 us
    ppermute x4, waiting for transfers between devices, sent(): return lax.ppermute(value, 'grp', pairs)  2.82 us
    pallas_call x1, Pallas kernels, shards(): pl.pallas_call(near_kernel, out_shape=[jax.ShapeDtypeStruct(part, jnp.flo...  1.89 us
    pallas_call x1, Pallas kernels, shards(): pl.pallas_call(mine_kernel, out_shape=[jax.ShapeDtypeStruct((far_tiles +...  1.39 us
    ppermute x2, waiting for transfers between devices, across(): return lax.ppermute(value, ('side', 'blk'), pairs)  1.34 us
  transfers between devices with their start and end apart: 9, of which 4 were waited for; matrix products, arithmetic and copies ran while one was open for 0% of the time, Pallas kernels for 23%

profile of v3, /device:TPU:0, one launch (start us, length us, event | category | flops | bytes accessed | tf_op | source)
XLA Modules:
  0.0 34.1 jit_solution(7718039610856025411)
XLA Ops:
  0.0 1.0 %shard_map.55 = (bf16[4,128,128]{2,1,0:T(8,128)(2,1)S(1)}, f32[4,128,128]{2,1,0:T(8,128)S(1)}) custom-call(s32[1,4]{1,0:T(1,128)} %exps_hbm.1, s32[1,512]{1,0:T(1,128)} %degrees_hbm.1, bf16[4,128,128]{2,1,0:T(8,128)(2,1)} %bitcast.7), custom_call_target="tpu_custom_call" | custom-call | flops 65536 | bytes 262144 | tf_op jit(solution)/shard_map/pallas_call | solution.py:51
  1.0 4.0 %collective-permute-start = (bf16[4,128,128]{2,1,0:T(8,128)(2,1)S(1)}, bf16[4,128,128]{2,1,0:T(8,128)(2,1)S(1)}, u32[]{:S(2)}, u32[]{:S(2)}) collective-permute-start(bf16[4,128,128]{2,1,0:T(8,128)(2,1)S(1)} %get-tuple-element.27), channel_id=1, source_target_pairs={{0,18},{1,19},{2,16},{3,17},{16,2},{17,3},{18,0},{19,1},{4,22},{5,... | collective-permute-start | bytes 393224 | tf_op jit(solution)/shard_map/ppermute | solution.py:233
  5.0 0.5 %collective-permute-start.1 = (bf16[4,128,128]{2,1,0:T(8,128)(2,1)S(1)}, bf16[4,128,128]{2,1,0:T(8,128)(2,1)S(1)}, u32[]{:S(2)}, u32[]{:S(2)}) collective-permute-start(bf16[4,128,128]{2,1,0:T(8,128)(2,1)S(1)} %get-tuple-element.27), channel_id=1, source_target_pairs={{0,16},{1,17},{2,18},{3,19},{16,0},{17,1},{18,2},{19,3},{4,20},{5,... | collective-permute-start | bytes 393224 | tf_op jit(solution)/shard_map/ppermute | solution.py:233
  5.5 0.1 pad_add_fusion.place_ref
  5.6 3.9 %shard_map.56 = (s32[5,112]{1,0:T(8,128)S(1)}, bf16[96,128,128]{2,1,0:T(8,128)(2,1)S(1)}) custom-call(s32[2]{0:T(128)S(1)} %pad_add_fusion.place_ref, s32[2,96]{1,0:T(2,128)} %bitcast.8, bf16[96,128,128]{2,1,0:T(8,128)(2,1)} %bitcast.6), custom_call_target="tpu_custom_call" | custom-call | tf_op jit(solution)/shard_map/pallas_call | solution.py:130
  9.5 0.0 collective-permute-done.panel.refs_0_
  9.5 0.1 collective-permute-start.2
  9.5 0.6 %shard_map.57.refs_4_ = f32[5,128,128]{2,1,0:T(8,128)S(1)} custom-call(s32[5,112]{1,0:T(8,128)S(1)} %get-tuple-element.36.order_ref, bf16[4,128,128]{2,1,0:T(8,128)(2,1)S(1)} %collective-permute-done.panel.refs_0_, bf16[96,128,128]{2,1,0:T(8,128)(2,1)S(1)} %get-tuple-element.31.blocks.refs_3_.refs_4_), custom_call_target="tpu_custom_call" | custom-call | flops 50331648 | bytes 393216 | tf_op jit(solution)/shard_map/pallas_call | solution.py:249
  10.2 1.3 %collective-permute-done.1.refs_0_.refs_1_ = bf16[4,128,128]{2,1,0:T(8,128)(2,1)S(1)} collective-permute-done((bf16[4,128,128]{2,1,0:T(8,128)(2,1)S(1)}, bf16[4,128,128]{2,1,0:T(8,128)(2,1)S(1)}, u32[]{:S(2)}, u32[]{:S(2)}) %collective-permute-start.1) | collective-permute-done | bytes 131104 | tf_op jit(solution)/shard_map/ppermute | solution.py:233
  11.5 0.0 collective-permute-start.3
  11.5 0.0 collective-permute-done.2.refs_1_.refs_2_
  11.5 1.3 %collective-permute-done.3.refs_2_.refs_3_ = bf16[4,128,128]{2,1,0:T(8,128)(2,1)S(1)} collective-permute-done((bf16[4,128,128]{2,1,0:T(8,128)(2,1)S(1)}, bf16[4,128,128]{2,1,0:T(8,128)(2,1)S(1)}, u32[]{:S(2)}, u32[]{:S(2)}) %collective-permute-start.3) | collective-permute-done | bytes 131104 | tf_op jit(solution)/shard_map/ppermute | solution.py:236
  12.9 1.1 %shard_map.58 = bf16[4,128,128]{2,1,0:T(8,128)(2,1)S(1)} custom-call(s32[5,112]{1,0:T(8,128)S(1)} %get-tuple-element.36.order_ref, bf16[4,128,128]{2,1,0:T(8,128)(2,1)S(1)} %collective-permute-done.1.refs_0_.refs_1_, bf16[4,128,128]{2,1,0:T(8,128)(2,1)S(1)} %collective-permute-done.2.refs_1_.refs_2_, ...), custom_call_target="tpu_custom_call" | custom-call | flops 50331648 | bytes 393216 | tf_op jit(solution)/shard_map/pallas_call | solution.py:259
  14.0 3.5 %collective-permute-start.6 = (bf16[4,128,128]{2,1,0:T(8,128)(2,1)S(1)}, bf16[4,128,128]{2,1,0:T(8,128)(2,1)S(1)}, u32[]{:S(2)}, u32[]{:S(2)}) collective-permute-start(bf16[4,128,128]{2,1,0:T(8,128)(2,1)S(1)} %shard_map.58), channel_id=1, source_target_pairs={{0,4},{12,8},{1,5},{13,9},{2,6},{14,10},{3,7},{15,11},{16,20},{28,... | collective-permute-start | bytes 393224 | tf_op jit(solution)/shard_map/ppermute | solution.py:304
  17.5 0.7 %collective-permute-start.4 = (bf16[4,128,128]{2,1,0:T(8,128)(2,1)S(1)}, bf16[4,128,128]{2,1,0:T(8,128)(2,1)S(1)}, u32[]{:S(2)}, u32[]{:S(2)}) collective-permute-start(bf16[4,128,128]{2,1,0:T(8,128)(2,1)S(1)} %shard_map.58), channel_id=1, source_target_pairs={{4,8},{8,4},{5,9},{9,5},{6,10},{10,6},{7,11},{11,7},{20,24},{24,20... | collective-permute-start | bytes 393224 | tf_op jit(solution)/shard_map/ppermute | solution.py:304
  18.2 1.4 %shard_map.59 = (f32[5,128,128]{2,1,0:T(8,128)S(1)}, bf16[4,128,128]{2,1,0:T(8,128)(2,1)S(1)}) custom-call(s32[5,112]{1,0:T(8,128)S(1)} %get-tuple-element.36.order_ref, bf16[4,128,128]{2,1,0:T(8,128)(2,1)S(1)} %collective-permute-done.panel.refs_0_, bf16[4,128,128]{2,1,0:T(8,128)(2,1)S(1)} %collective-permute-done.1.refs_0_.refs_1_, ...), custom_call_target="tpu_custom_call" | custom-call | flops 100663296 | bytes 786432 | tf_op jit(solution)/shard_map/pallas_call | solution.py:270
  19.5 4.0 %collective-permute-start.5 = (bf16[4,128,128]{2,1,0:T(8,128)(2,1)S(1)}, bf16[4,128,128]{2,1,0:T(8,128)(2,1)S(1)}, u32[]{:S(2)}, u32[]{:S(2)}) collective-permute-start(bf16[4,128,128]{2,1,0:T(8,128)(2,1)S(1)} %get-tuple-element.39), channel_id=1, source_target_pairs={{0,8},{12,4},{1,9},{13,5},{2,10},{14,6},{3,11},{15,7},{16,24},{28,... | collective-permute-start | bytes 393224 | tf_op jit(solution)/shard_map/ppermute | solution.py:304
  23.5 1.9 %shard_map.60 = (f32[4,128,128]{2,1,0:T(8,128)S(1)}, bf16[4,128,128]{2,1,0:T(8,128)(2,1)S(1)}) custom-call(s32[5,112]{1,0:T(8,128)S(1)} %get-tuple-element.36.order_ref, bf16[4,128,128]{2,1,0:T(8,128)(2,1)S(1)} %collective-permute-done.panel.refs_0_, bf16[4,128,128]{2,1,0:T(8,128)(2,1)S(1)} %collective-permute-done.1.refs_0_.refs_1_, ...), custom_call_target="tpu_custom_call" | custom-call | flops 201326592 | bytes 1572864 | tf_op jit(solution)/shard_map/pallas_call | solution.py:283
  25.4 0.0 collective-permute-done.6
  25.5 0.1 collective-permute-start.7
  25.6 1.3 %collective-permute-start.8 = (bf16[4,128,128]{2,1,0:T(8,128)(2,1)S(1)}, bf16[4,128,128]{2,1,0:T(8,128)(2,1)S(1)}, u32[]{:S(2)}, u32[]{:S(2)}) collective-permute-start(bf16[4,128,128]{2,1,0:T(8,128)(2,1)S(1)} %add_convert_fusion), channel_id=1, source_target_pairs={{4,12},{8,0},{5,13},{9,1},{6,14},{10,2},{7,15},{11,3},{20,28},{24,... | collective-permute-start | bytes 393224 | tf_op jit(solution)/shard_map/ppermute | solution.py:304
  26.9 3.7 %collective-permute-done.7.refs_0_ = bf16[4,128,128]{2,1,0:T(8,128)(2,1)S(1)} collective-permute-done((bf16[4,128,128]{2,1,0:T(8,128)(2,1)S(1)}, bf16[4,128,128]{2,1,0:T(8,128)(2,1)S(1)}, u32[]{:S(2)}, u32[]{:S(2)}) %collective-permute-start.7) | collective-permute-done | bytes 131104 | tf_op jit(solution)/shard_map/ppermute | solution.py:236
  30.6 2.8 %collective-permute-done.8.refs_1_ = bf16[4,128,128]{2,1,0:T(8,128)(2,1)S(1)} collective-permute-done((bf16[4,128,128]{2,1,0:T(8,128)(2,1)S(1)}, bf16[4,128,128]{2,1,0:T(8,128)(2,1)S(1)}, u32[]{:S(2)}, u32[]{:S(2)}) %collective-permute-start.8) | collective-permute-done | bytes 131104 | tf_op jit(solution)/shard_map/ppermute | solution.py:304
  33.4 0.7 %shard_map.61 = bf16[4,128,128]{2,1,0:T(8,128)(2,1)} custom-call(f32[4,128,128]{2,1,0:T(8,128)S(1)} %get-tuple-element.26.factors, f32[4,128,128]{2,1,0:T(8,128)S(1)} %add_add_fusion.own, bf16[4,128,128]{2,1,0:T(8,128)(2,1)S(1)} %collective-permute-done.7.refs_0_, bf16[4,128,128]{2,1,0:T(8,128)(2,1)S(1)} %collective-permute-done.8.refs_1_), custom_call_target="tpu_custom_call" | custom-call | tf_op jit(solution)/shard_map/pallas_call | solution.py:318
  (4 shorter events, 0.1 us)
Async XLA Ops:
  1.0 8.5 %collective-permute-start = (bf16[4,128,128]{2,1,0:T(8,128)(2,1)S(1)}, bf16[4,128,128]{2,1,0:T(8,128)(2,1)S(1)}, u32[]{:S(2)}, u32[]{:S(2)}) collective-permute-start(bf16[4,128,128]{2,1,0:T(8,128)(2,1)S(1)} %get-tuple-element.27), channel_id=1, source_target_pairs={{0,18},{1,19},{2,16},{3,17},{16,2},{17,3},{18,0},{19,1},{4,22},{5,... | collective-permute-start | bytes 393224 | tf_op jit(solution)/shard_map/ppermute | solution.py:233
  5.0 6.6 %collective-permute-start.1 = (bf16[4,128,128]{2,1,0:T(8,128)(2,1)S(1)}, bf16[4,128,128]{2,1,0:T(8,128)(2,1)S(1)}, u32[]{:S(2)}, u32[]{:S(2)}) collective-permute-start(bf16[4,128,128]{2,1,0:T(8,128)(2,1)S(1)} %get-tuple-element.27), channel_id=1, source_target_pairs={{0,16},{1,17},{2,18},{3,19},{16,0},{17,1},{18,2},{19,3},{4,20},{5,... | collective-permute-start | bytes 393224 | tf_op jit(solution)/shard_map/ppermute | solution.py:233
  9.5 2.1 %collective-permute-start.2 = (bf16[4,128,128]{2,1,0:T(8,128)(2,1)S(1)}, bf16[4,128,128]{2,1,0:T(8,128)(2,1)S(1)}, u32[]{:S(2)}, u32[]{:S(2)}) collective-permute-start(bf16[4,128,128]{2,1,0:T(8,128)(2,1)S(1)} %collective-permute-done.panel.refs_0_), channel_id=1, source_target_pairs={{0,1},{1,0},{2,3},{3,2},{4,5},{5,4},{6,7},{7,6},{8,9},{9,8},{10,11... | collective-permute-start | bytes 393224 | tf_op jit(solution)/shard_map/ppermute | solution.py:236
  11.5 1.3 %collective-permute-start.3 = (bf16[4,128,128]{2,1,0:T(8,128)(2,1)S(1)}, bf16[4,128,128]{2,1,0:T(8,128)(2,1)S(1)}, u32[]{:S(2)}, u32[]{:S(2)}) collective-permute-start(bf16[4,128,128]{2,1,0:T(8,128)(2,1)S(1)} %collective-permute-done.1.refs_0_.refs_1_), channel_id=1, source_target_pairs={{0,1},{1,0},{2,3},{3,2},{4,5},{5,4},{6,7},{7,6},{8,9},{9,8},{10,11... | collective-permute-start | bytes 393224 | tf_op jit(solution)/shard_map/ppermute | solution.py:236
  14.0 11.5 %collective-permute-start.6 = (bf16[4,128,128]{2,1,0:T(8,128)(2,1)S(1)}, bf16[4,128,128]{2,1,0:T(8,128)(2,1)S(1)}, u32[]{:S(2)}, u32[]{:S(2)}) collective-permute-start(bf16[4,128,128]{2,1,0:T(8,128)(2,1)S(1)} %shard_map.58), channel_id=1, source_target_pairs={{0,4},{12,8},{1,5},{13,9},{2,6},{14,10},{3,7},{15,11},{16,20},{28,... | collective-permute-start | bytes 393224 | tf_op jit(solution)/shard_map/ppermute | solution.py:304
  17.5 9.4 %collective-permute-start.4 = (bf16[4,128,128]{2,1,0:T(8,128)(2,1)S(1)}, bf16[4,128,128]{2,1,0:T(8,128)(2,1)S(1)}, u32[]{:S(2)}, u32[]{:S(2)}) collective-permute-start(bf16[4,128,128]{2,1,0:T(8,128)(2,1)S(1)} %shard_map.58), channel_id=1, source_target_pairs={{4,8},{8,4},{5,9},{9,5},{6,10},{10,6},{7,11},{11,7},{20,24},{24,20... | collective-permute-start | bytes 393224 | tf_op jit(solution)/shard_map/ppermute | solution.py:304
  19.5 7.3 %collective-permute-start.5 = (bf16[4,128,128]{2,1,0:T(8,128)(2,1)S(1)}, bf16[4,128,128]{2,1,0:T(8,128)(2,1)S(1)}, u32[]{:S(2)}, u32[]{:S(2)}) collective-permute-start(bf16[4,128,128]{2,1,0:T(8,128)(2,1)S(1)} %get-tuple-element.39), channel_id=1, source_target_pairs={{0,8},{12,4},{1,9},{13,5},{2,10},{14,6},{3,11},{15,7},{16,24},{28,... | collective-permute-start | bytes 393224 | tf_op jit(solution)/shard_map/ppermute | solution.py:304
  25.5 5.1 %collective-permute-start.7 = (bf16[4,128,128]{2,1,0:T(8,128)(2,1)S(1)}, bf16[4,128,128]{2,1,0:T(8,128)(2,1)S(1)}, u32[]{:S(2)}, u32[]{:S(2)}) collective-permute-start(bf16[4,128,128]{2,1,0:T(8,128)(2,1)S(1)} %get-tuple-element.42), channel_id=1, source_target_pairs={{0,4},{4,0},{8,12},{12,8},{1,5},{5,1},{9,13},{13,9},{2,6},{6,2},{1... | collective-permute-start | bytes 393224 | tf_op jit(solution)/shard_map/ppermute | solution.py:236
  25.6 7.9 %collective-permute-start.8 = (bf16[4,128,128]{2,1,0:T(8,128)(2,1)S(1)}, bf16[4,128,128]{2,1,0:T(8,128)(2,1)S(1)}, u32[]{:S(2)}, u32[]{:S(2)}) collective-permute-start(bf16[4,128,128]{2,1,0:T(8,128)(2,1)S(1)} %add_convert_fusion), channel_id=1, source_target_pairs={{4,12},{8,0},{5,13},{9,1},{6,14},{10,2},{7,15},{11,3},{20,28},{24,... | collective-permute-start | bytes 393224 | tf_op jit(solution)/shard_map/ppermute | solution.py:304

commit v4 on v3

--- a/solution.py
+++ b/solution.py
@@ -8,7 +8,7 @@
 from jax.sharding import PartitionSpec as P
 
 UNROLL = 8
-STAGES = 4
+STAGES = 3
 VMEM = pl.BlockSpec(memory_space=pltpu.VMEM)
 SMEM = pl.BlockSpec(memory_space=pltpu.SMEM)
 HBM = pl.BlockSpec(memory_space=pltpu.HBM)
@@ -82,6 +82,7 @@
     capacity = index_ref.shape[1]
     source_tiles = blks * tiles_dev
     half = blks // 2
+    role = my_blk & 1
 
     def enlist(slot, nexts):
         target = index_ref[0, slot]
@@ -93,10 +94,11 @@
         rank = half - 1 - (hop >> 1)
         odd = hop & 1
         far = (chunk >= 2) & ((chunk & 1) == 1)
-        stage = jnp.where(far, jnp.minimum(rank + odd, 1), jnp.where(chunk >= 2, 2, 3))
+        stage = jnp.where(far, jnp.minimum(rank + odd, 1), 2)
         stage = jnp.where(origin < source_tiles, stage, STAGES)
         panel = rank + odd * half - (stage == 1).astype(jnp.int32)
-        kept = jnp.where(chunk >= 2, (chunk >> 1) - 1, chunk)
+        kept = jnp.where(chunk == 1, 1 + role * (groups // 2 - 1), (chunk >> 1) + 1 - role)
+        kept = jnp.where(chunk == 0, 0, jnp.where(far, (chunk >> 1) - 1, kept))
         word = pack(slot, panel * tiles_dev + row, kept * tiles_dev + tile)
         where = jnp.int32(0)
         for at, position in enumerate(nexts):
@@ -108,7 +110,7 @@
 
     ends = lax.fori_loop(0, capacity, enlist, (jnp.int32(0),) * STAGES, unroll=8)
     far_tiles = (groups // 2 - 1) * tiles_dev
-    spares = [pack(0, 0, far_tiles)] * 3 + [pack(0, 0, 2 * tiles_dev)]
+    spares = [pack(0, 0, far_tiles)] * 2 + [pack(0, 0, (groups // 2 + 1) * tiles_dev)]
     for at, (end, spare) in enumerate(zip(ends, spares)):
         for extra in range(UNROLL):
             order_ref[at, end + extra] = spare
@@ -174,21 +176,15 @@
     far[...] = total[: far.shape[0]].astype(far.dtype)
 
 
-def mine_kernel(order_ref, *refs):
-    *panels, blocks, total, mine, source = refs
+def rest_kernel(order_ref, *refs):
+    *panels, blocks, own, first, later, source, total = refs
     gather_panels(panels, source)
     total[...] = jnp.zeros_like(total)
     add_products(2, order_ref, blocks, source, total)
-    mine[...] = total[: mine.shape[0]].astype(mine.dtype)
-
-
-def near_kernel(order_ref, *refs):
-    *panels, blocks, own, near, source, total = refs
-    gather_panels(panels, source)
-    total[...] = jnp.zeros_like(total)
-    add_products(3, order_ref, blocks, source, total)
-    own[...] = total[: own.shape[0]]
-    near[...] = total[own.shape[0] : 2 * own.shape[0]].astype(near.dtype)
+    tiles_dev = own.shape[0]
+    own[...] = total[:tiles_dev]
+    first[...] = total[tiles_dev : 2 * tiles_dev].astype(first.dtype)
+    later[...] = total[2 * tiles_dev : 2 * tiles_dev + later.shape[0]]
 
 
 def final_kernel(factors, own, *refs):
@@ -240,8 +236,7 @@
     order, blocks = stage_blocks(block_index[0], place, adjacency[0], blks, groups, tiles_dev)
     early, order = lax.optimization_barrier((early, order))
     other = paired(early, "blk", 1)
-    far_chunks, mine_chunks = range(3, groups, 2), range(2, groups, 2)
-    far_tiles = len(far_chunks) * tiles_dev
+    far_tiles = (groups // 2 - 1) * tiles_dev
 
     def held(count, dtype):
         return pltpu.VMEM((count, tile_rows, row_width), dtype)
@@ -267,58 +262,54 @@
     )(order, *panels, blocks, total)
     far, order = lax.optimization_barrier((far, order))
     panels = [early] + panels
-    mine_total, mine = pl.pallas_call(
-        mine_kernel,
-        out_shape=[
-            jax.ShapeDtypeStruct((far_tiles + 1, tile_rows, row_width), jnp.float32),
-            jax.ShapeDtypeStruct((far_tiles, tile_rows, row_width), jnp.bfloat16),
-        ],
-        in_specs=[SMEM] + [VMEM] * (len(panels) + 1),
-        out_specs=[VMEM] * 2,
-        scratch_shapes=[held(len(panels) * tiles_dev, jnp.bfloat16)],
-        compiler_params=LIMIT,
-        cost_estimate=cost_of(capacity // 4, tile_rows, row_width),
-    )(order, *panels, blocks)
-    mine, order = lax.optimization_barrier((mine, order))
-    own, near = pl.pallas_call(
-        near_kernel,
+    own, first, later = pl.pallas_call(
+        rest_kernel,
         out_shape=[
             jax.ShapeDtypeStruct(part, jnp.float32),
             jax.ShapeDtypeStruct(part, jnp.bfloat16),
+            jax.ShapeDtypeStruct((far_tiles, tile_rows, row_width), jnp.float32),
         ],
         in_specs=[SMEM] + [VMEM] * (len(panels) + 1),
-        out_specs=[VMEM] * 2,
+        out_specs=[VMEM] * 3,
         scratch_shapes=[
             held(len(panels) * tiles_dev, jnp.bfloat16),
-            held(2 * tiles_dev + 1, jnp.float32),
-        ],
-        compiler_params=LIMIT,
-        cost_estimate=cost_of(capacity // 2, tile_rows, row_width),
+            held((groups // 2 + 1) * tiles_dev + 1, jnp.float32),
+        ],
+        compiler_params=LIMIT,
+        cost_estimate=cost_of(capacity, tile_rows, row_width),
     )(order, *panels, blocks)
 
-    def outer(at, owner):
-        return abs(at - owner) > abs((at ^ 1) - owner)
-
-    def sent(value, way, hop, wanted):
-        pairs = [(at, at ^ way) for at in range(groups) if outer(at, at ^ hop) == wanted]
-        return lax.ppermute(value, "grp", pairs)
-
-    straight, sums = [], []
-    for at, hop in enumerate(mine_chunks):
-        piece = slice(at * tiles_dev, (at + 1) * tiles_dev)
-        handed = sent(far[piece], 1, hop + 1, True)
-        straight.append(sent(far[piece], hop + 1, hop + 1, False))
-        straight.append(sent(mine[piece], hop, hop, True))
-        pair = (mine_total[piece] + handed.astype(jnp.float32)).astype(jnp.bfloat16)
-        near, pair = lax.optimization_barrier((near, pair))
-        sums.append(sent(pair, hop, hop, False))
-    near_arrived = paired(near, "grp", 1)
-    own = own + sum(piece.astype(jnp.float32) for piece in straight)
-    own, near_arrived, *sums = lax.optimization_barrier((own, near_arrived, *sums))
+    def turned(value, even_hop, odd_hop):
+        hops = (even_hop, odd_hop)
+        pairs = [
+            (at * blks + blk, (at ^ hops[blk & 1]) * blks + blk)
+            for at in range(groups)
+            for blk in range(blks)
+        ]
+        return lax.ppermute(value, ("grp", "blk"), pairs)
+
+    steps = groups // 2 - 1
+    even_core = lax.axis_index("blk") % 2 == 0
+    pieces = [slice(at * tiles_dev, (at + 1) * tiles_dev) for at in range(steps)]
+    handed = [turned(far[pieces[at]], 1, 2 * at + 2).astype(jnp.float32) for at in range(steps)]
+    arrived = [turned(first, 1, 2)]
+    for at in range(steps):
+        value = later[pieces[at]]
+        for step, extra in enumerate(handed):
+            if step == at == steps - 1:
+                value = value + extra
+            elif step == at:
+                value = value + jnp.where(even_core, extra, 0.0)
+            elif at == steps - 1:
+                value = value + jnp.where(even_core, 0.0, extra)
+        odd_hop = 1 if at == steps - 1 else 2 * at + 4
+        arrived.append(turned(value.astype(jnp.bfloat16), 2 * at + 2, odd_hop))
+    own = own + arrived[0].astype(jnp.float32)
+    own, *sums = lax.optimization_barrier((own, *arrived[1:]))
     out = pl.pallas_call(
         final_kernel,
         out_shape=jax.ShapeDtypeStruct(part, jnp.bfloat16),
-        in_specs=[VMEM] * (3 + len(sums)),
+        in_specs=[VMEM] * (2 + len(sums)),
         out_specs=HBM,
         scratch_shapes=[
             held(tiles_dev, jnp.bfloat16),
@@ -326,7 +317,7 @@
         ],
         compiler_params=LIMIT,
         cost_estimate=cost_of(0, tile_rows, row_width),
-    )(factors, own, near_arrived, *sums)
+    )(factors, own, *sums)
     return out.reshape(1, row_count, row_width)
 
 

time: 34.2 us -> 28.4 us (0.83)
  starting transfers between devices: 14.1 us -> 8.9 us
  Pallas kernels: 10.6 us -> 9.81 us
  waiting for transfers between devices: 9.19 us -> 9.66 us
    ppermute x4 -> x3, starting transfers between devices: 9.43 us -> 4.33 us  [turned(): return lax.ppermute(value, ('grp', 'blk'), pairs)]
    ppermute x4 -> x3, waiting for transfers between devices: 2.82 us -> 7.4 us  [turned(): return lax.ppermute(value, ('grp', 'blk'), pairs)]
    ppermute x3 -> x2, waiting for transfers between devices: 5.04 us -> 1.34 us  [paired(): lax.ppermute(value, axis, [(at, at ^ hop) for at in range(lax.axis_size(a...]
    pallas_call x2 -> x1, Pallas kernels: 3.27 us -> 2.12 us  [shards(): pl.pallas_call(rest_kernel, out_shape=[jax.ShapeDtypeStruct(part, jnp.flo...]
    pallas_call x1, Pallas kernels: 0.62 us -> 1.07 us  [shards(): pl.pallas_call(early_kernel, out_shape=jax.ShapeDtypeStruct((far_tiles +...]
    ppermute x2, waiting for transfers between devices: 1.34 us -> 0.91 us  [across(): return lax.ppermute(value, ('side', 'blk'), pairs)]
  transfers between devices with their start and end apart: 9 -> 7, of which waited for: 4 -> 5; matrix products, arithmetic and copies ran while one was open for 0% -> 0% of each run, Pallas kernels for 23% -> 25%
where the time goes in v4:
time: 28.4 us; the launch traced here: 28.6 us
  Pallas kernels  9.81 us (35%)
  waiting for transfers between devices  9.66 us (34%)
  starting transfers between devices  8.9 us (31%)
    ppermute x3, waiting for transfers between devices, turned(): return lax.ppermute(value, ('grp', 'blk'), pairs)  7.4 us
    ppermute x2, starting transfers between devices, across(): return lax.ppermute(value, ('side', 'blk'), pairs)  4.49 us
    ppermute x3, starting transfers between devices, turned(): return lax.ppermute(value, ('grp', 'blk'), pairs)  4.33 us
    pallas_call x1, Pallas kernels, stage_blocks(): pl.pallas_call(functools.partial(stage_kernel, blks, groups, tiles_dev),...  3.86 us
    pallas_call x1, Pallas kernels, shards(): pl.pallas_call(rest_kernel, out_shape=[jax.ShapeDtypeStruct(part, jnp.flo...  2.12 us
    ppermute x2, waiting for transfers between devices, paired(): lax.ppermute(value, axis, [(at, at ^ hop) for at in range(lax.axis_size(a...  1.34 us
    pallas_call x1, Pallas kernels, shards(): pl.pallas_call(far_kernel, out_shape=jax.ShapeDtypeStruct((far_tiles, til...  1.09 us
    pallas_call x1, Pallas kernels, shards(): pl.pallas_call(early_kernel, out_shape=jax.ShapeDtypeStruct((far_tiles +...  1.07 us
  transfers between devices with their start and end apart: 7, of which 5 were waited for; matrix products, arithmetic and copies ran while one was open for 0% of the time, Pallas kernels for 25%

profile of v4, /device:TPU:0, one launch (start us, length us, event | category | flops | bytes accessed | tf_op | source)
XLA Modules:
  0.0 28.6 jit_solution(9505981371429867346)
XLA Ops:
  0.0 1.0 %shard_map.55 = (bf16[4,128,128]{2,1,0:T(8,128)(2,1)S(1)}, f32[4,128,128]{2,1,0:T(8,128)S(1)}) custom-call(s32[1,4]{1,0:T(1,128)} %exps_hbm.1, s32[1,512]{1,0:T(1,128)} %degrees_hbm.1, bf16[4,128,128]{2,1,0:T(8,128)(2,1)} %bitcast.7), custom_call_target="tpu_custom_call" | custom-call | flops 65536 | bytes 262144 | tf_op jit(solution)/shard_map/pallas_call | solution.py:51
  1.0 4.0 %collective-permute-start = (bf16[4,128,128]{2,1,0:T(8,128)(2,1)S(1)}, bf16[4,128,128]{2,1,0:T(8,128)(2,1)S(1)}, u32[]{:S(2)}, u32[]{:S(2)}) collective-permute-start(bf16[4,128,128]{2,1,0:T(8,128)(2,1)S(1)} %get-tuple-element.21), channel_id=1, source_target_pairs={{0,18},{1,19},{2,16},{3,17},{16,2},{17,3},{18,0},{19,1},{4,22},{5,... | collective-permute-start | bytes 393224 | tf_op jit(solution)/shard_map/ppermute | solution.py:229
  5.0 0.5 %collective-permute-start.1 = (bf16[4,128,128]{2,1,0:T(8,128)(2,1)S(1)}, bf16[4,128,128]{2,1,0:T(8,128)(2,1)S(1)}, u32[]{:S(2)}, u32[]{:S(2)}) collective-permute-start(bf16[4,128,128]{2,1,0:T(8,128)(2,1)S(1)} %get-tuple-element.21), channel_id=1, source_target_pairs={{0,16},{1,17},{2,18},{3,19},{16,0},{17,1},{18,2},{19,3},{4,20},{5,... | collective-permute-start | bytes 393224 | tf_op jit(solution)/shard_map/ppermute | solution.py:229
  5.5 0.1 pad_add_fusion.place_ref
  5.6 3.9 %shard_map.56 = (s32[4,112]{1,0:T(4,128)S(1)}, bf16[96,128,128]{2,1,0:T(8,128)(2,1)S(1)}) custom-call(s32[2]{0:T(128)S(1)} %pad_add_fusion.place_ref, s32[2,96]{1,0:T(2,128)} %bitcast.8, bf16[96,128,128]{2,1,0:T(8,128)(2,1)} %bitcast.6), custom_call_target="tpu_custom_call" | custom-call | tf_op jit(solution)/shard_map/pallas_call | solution.py:132
  9.4 0.0 collective-permute-done.panel.refs_0_
  9.4 0.1 collective-permute-start.2
  9.5 1.1 %shard_map.57.refs_4_ = f32[5,128,128]{2,1,0:T(8,128)S(1)} custom-call(s32[4,112]{1,0:T(4,128)S(1)} %get-tuple-element.28.order_ref, bf16[4,128,128]{2,1,0:T(8,128)(2,1)S(1)} %collective-permute-done.panel.refs_0_, bf16[96,128,128]{2,1,0:T(8,128)(2,1)S(1)} %get-tuple-element.25.blocks.refs_3_.refs_4_), custom_call_target="tpu_custom_call" | custom-call | flops 50331648 | bytes 393216 | tf_op jit(solution)/shard_map/pallas_call | solution.py:244
  10.6 0.9 %collective-permute-done.1.refs_0_.refs_1_ = bf16[4,128,128]{2,1,0:T(8,128)(2,1)S(1)} collective-permute-done((bf16[4,128,128]{2,1,0:T(8,128)(2,1)S(1)}, bf16[4,128,128]{2,1,0:T(8,128)(2,1)S(1)}, u32[]{:S(2)}, u32[]{:S(2)}) %collective-permute-start.1) | collective-permute-done | bytes 131104 | tf_op jit(solution)/shard_map/ppermute | solution.py:229
  11.5 0.0 collective-permute-start.3
  11.5 0.0 collective-permute-done.2.refs_1_.refs_2_
  11.5 1.3 %collective-permute-done.3.refs_2_.refs_3_ = bf16[4,128,128]{2,1,0:T(8,128)(2,1)S(1)} collective-permute-done((bf16[4,128,128]{2,1,0:T(8,128)(2,1)S(1)}, bf16[4,128,128]{2,1,0:T(8,128)(2,1)S(1)}, u32[]{:S(2)}, u32[]{:S(2)}) %collective-permute-start.3) | collective-permute-done | bytes 131104 | tf_op jit(solution)/shard_map/ppermute | solution.py:232
  12.9 1.1 %shard_map.58 = bf16[4,128,128]{2,1,0:T(8,128)(2,1)S(1)} custom-call(s32[4,112]{1,0:T(4,128)S(1)} %get-tuple-element.28.order_ref, bf16[4,128,128]{2,1,0:T(8,128)(2,1)S(1)} %collective-permute-done.1.refs_0_.refs_1_, bf16[4,128,128]{2,1,0:T(8,128)(2,1)S(1)} %collective-permute-done.2.refs_1_.refs_2_, ...), custom_call_target="tpu_custom_call" | custom-call | flops 50331648 | bytes 393216 | tf_op jit(solution)/shard_map/pallas_call | solution.py:254
  14.0 1.9 %collective-permute-start.5 = (bf16[4,128,128]{2,1,0:T(8,128)(2,1)S(1)}, bf16[4,128,128]{2,1,0:T(8,128)(2,1)S(1)}, u32[]{:S(2)}, u32[]{:S(2)}) collective-permute-start(bf16[4,128,128]{2,1,0:T(8,128)(2,1)S(1)} %shard_map.58), channel_id=1, source_target_pairs={{0,4},{1,9},{2,6},{3,11},{4,0},{5,13},{6,2},{7,15},{8,12},{9,1},{1... | collective-permute-start | bytes 393224 | tf_op jit(solution)/shard_map/ppermute | solution.py:289
  15.8 2.1 %shard_map.59 = (f32[4,128,128]{2,1,0:T(8,128)S(1)}, bf16[4,128,128]{2,1,0:T(8,128)(2,1)S(1)}, f32[4,128,128]{2,1,0:T(8,128)S(1)}) custom-call(s32[4,112]{1,0:T(4,128)S(1)} %get-tuple-element.28.order_ref, bf16[4,128,128]{2,1,0:T(8,128)(2,1)S(1)} %collective-permute-done.panel.refs_0_, bf16[4,128,128]{2,1,0:T(8,128)(2,1)S(1)} %collective-permute-done.1.refs_0_.refs_1_, ...), custom_call_target="tpu_custom_call" | custom-call | flops 402653184 | bytes 3145728 | tf_op jit(solution)/shard_map/pallas_call | solution.py:265
  17.9 0.5 %collective-permute-start.4 = (bf16[4,128,128]{2,1,0:T(8,128)(2,1)S(1)}, bf16[4,128,128]{2,1,0:T(8,128)(2,1)S(1)}, u32[]{:S(2)}, u32[]{:S(2)}) collective-permute-start(bf16[4,128,128]{2,1,0:T(8,128)(2,1)S(1)} %get-tuple-element.30), channel_id=1, source_target_pairs={{0,4},{1,9},{2,6},{3,11},{4,0},{5,13},{6,2},{7,15},{8,12},{9,1},{1... | collective-permute-start | bytes 393224 | tf_op jit(solution)/shard_map/ppermute | solution.py:289
  18.5 1.9 %collective-permute-done.5 = bf16[4,128,128]{2,1,0:T(8,128)(2,1)S(1)} collective-permute-done((bf16[4,128,128]{2,1,0:T(8,128)(2,1)S(1)}, bf16[4,128,128]{2,1,0:T(8,128)(2,1)S(1)}, u32[]{:S(2)}, u32[]{:S(2)}) %collective-permute-start.5) | collective-permute-done | bytes 131104 | tf_op jit(solution)/shard_map/ppermute | solution.py:289
  20.4 1.9 %collective-permute-start.6 = (bf16[4,128,128]{2,1,0:T(8,128)(2,1)S(1)}, bf16[4,128,128]{2,1,0:T(8,128)(2,1)S(1)}, u32[]{:S(2)}, u32[]{:S(2)}) collective-permute-start(bf16[4,128,128]{2,1,0:T(8,128)(2,1)S(1)} %add_convert_fusion), channel_id=1, source_target_pairs={{0,8},{1,5},{2,10},{3,7},{4,12},{5,1},{6,14},{7,3},{8,0},{9,13},{1... | collective-permute-start | bytes 393224 | tf_op jit(solution)/shard_map/ppermute | solution.py:289
  22.4 2.3 %collective-permute-done.4 = bf16[4,128,128]{2,1,0:T(8,128)(2,1)S(1)} collective-permute-done((bf16[4,128,128]{2,1,0:T(8,128)(2,1)S(1)}, bf16[4,128,128]{2,1,0:T(8,128)(2,1)S(1)}, u32[]{:S(2)}, u32[]{:S(2)}) %collective-permute-start.4) | collective-permute-done | bytes 131104 | tf_op jit(solution)/shard_map/ppermute | solution.py:289
  24.7 3.2 %collective-permute-done.6.refs_0_ = bf16[4,128,128]{2,1,0:T(8,128)(2,1)S(1)} collective-permute-done((bf16[4,128,128]{2,1,0:T(8,128)(2,1)S(1)}, bf16[4,128,128]{2,1,0:T(8,128)(2,1)S(1)}, u32[]{:S(2)}, u32[]{:S(2)}) %collective-permute-start.6) | collective-permute-done | bytes 131104 | tf_op jit(solution)/shard_map/ppermute | solution.py:289
  27.9 0.7 %shard_map.60 = bf16[4,128,128]{2,1,0:T(8,128)(2,1)} custom-call(f32[4,128,128]{2,1,0:T(8,128)S(1)} %get-tuple-element.20.factors, f32[4,128,128]{2,1,0:T(8,128)S(1)} %convert_add_fusion.own, bf16[4,128,128]{2,1,0:T(8,128)(2,1)S(1)} %collective-permute-done.6.refs_0_), custom_call_target="tpu_custom_call" | custom-call | tf_op jit(solution)/shard_map/pallas_call | solution.py:309
  (2 shorter events, 0.1 us)
Async XLA Ops:
  1.0 8.4 %collective-permute-start = (bf16[4,128,128]{2,1,0:T(8,128)(2,1)S(1)}, bf16[4,128,128]{2,1,0:T(8,128)(2,1)S(1)}, u32[]{:S(2)}, u32[]{:S(2)}) collective-permute-start(bf16[4,128,128]{2,1,0:T(8,128)(2,1)S(1)} %get-tuple-element.21), channel_id=1, source_target_pairs={{0,18},{1,19},{2,16},{3,17},{16,2},{17,3},{18,0},{19,1},{4,22},{5,... | collective-permute-start | bytes 393224 | tf_op jit(solution)/shard_map/ppermute | solution.py:229
  5.0 6.6 %collective-permute-start.1 = (bf16[4,128,128]{2,1,0:T(8,128)(2,1)S(1)}, bf16[4,128,128]{2,1,0:T(8,128)(2,1)S(1)}, u32[]{:S(2)}, u32[]{:S(2)}) collective-permute-start(bf16[4,128,128]{2,1,0:T(8,128)(2,1)S(1)} %get-tuple-element.21), channel_id=1, source_target_pairs={{0,16},{1,17},{2,18},{3,19},{16,0},{17,1},{18,2},{19,3},{4,20},{5,... | collective-permute-start | bytes 393224 | tf_op jit(solution)/shard_map/ppermute | solution.py:229
  9.4 2.1 %collective-permute-start.2 = (bf16[4,128,128]{2,1,0:T(8,128)(2,1)S(1)}, bf16[4,128,128]{2,1,0:T(8,128)(2,1)S(1)}, u32[]{:S(2)}, u32[]{:S(2)}) collective-permute-start(bf16[4,128,128]{2,1,0:T(8,128)(2,1)S(1)} %collective-permute-done.panel.refs_0_), channel_id=1, source_target_pairs={{0,1},{1,0},{2,3},{3,2},{4,5},{5,4},{6,7},{7,6},{8,9},{9,8},{10,11... | collective-permute-start | bytes 393224 | tf_op jit(solution)/shard_map/ppermute | solution.py:232
  11.5 1.3 %collective-permute-start.3 = (bf16[4,128,128]{2,1,0:T(8,128)(2,1)S(1)}, bf16[4,128,128]{2,1,0:T(8,128)(2,1)S(1)}, u32[]{:S(2)}, u32[]{:S(2)}) collective-permute-start(bf16[4,128,128]{2,1,0:T(8,128)(2,1)S(1)} %collective-permute-done.1.refs_0_.refs_1_), channel_id=1, source_target_pairs={{0,1},{1,0},{2,3},{3,2},{4,5},{5,4},{6,7},{7,6},{8,9},{9,8},{10,11... | collective-permute-start | bytes 393224 | tf_op jit(solution)/shard_map/ppermute | solution.py:232
  14.0 6.4 %collective-permute-start.5 = (bf16[4,128,128]{2,1,0:T(8,128)(2,1)S(1)}, bf16[4,128,128]{2,1,0:T(8,128)(2,1)S(1)}, u32[]{:S(2)}, u32[]{:S(2)}) collective-permute-start(bf16[4,128,128]{2,1,0:T(8,128)(2,1)S(1)} %shard_map.58), channel_id=1, source_target_pairs={{0,4},{1,9},{2,6},{3,11},{4,0},{5,13},{6,2},{7,15},{8,12},{9,1},{1... | collective-permute-start | bytes 393224 | tf_op jit(solution)/shard_map/ppermute | solution.py:289
  17.9 6.7 %collective-permute-start.4 = (bf16[4,128,128]{2,1,0:T(8,128)(2,1)S(1)}, bf16[4,128,128]{2,1,0:T(8,128)(2,1)S(1)}, u32[]{:S(2)}, u32[]{:S(2)}) collective-permute-start(bf16[4,128,128]{2,1,0:T(8,128)(2,1)S(1)} %get-tuple-element.30), channel_id=1, source_target_pairs={{0,4},{1,9},{2,6},{3,11},{4,0},{5,13},{6,2},{7,15},{8,12},{9,1},{1... | collective-permute-start | bytes 393224 | tf_op jit(solution)/shard_map/ppermute | solution.py:289
  20.4 7.5 %collective-permute-start.6 = (bf16[4,128,128]{2,1,0:T(8,128)(2,1)S(1)}, bf16[4,128,128]{2,1,0:T(8,128)(2,1)S(1)}, u32[]{:S(2)}, u32[]{:S(2)}) collective-permute-start(bf16[4,128,128]{2,1,0:T(8,128)(2,1)S(1)} %add_convert_fusion), channel_id=1, source_target_pairs={{0,8},{1,5},{2,10},{3,7},{4,12},{5,1},{6,14},{7,3},{8,0},{9,13},{1... | collective-permute-start | bytes 393224 | tf_op jit(solution)/shard_map/ppermute | solution.py:289
